TPU v7x, 256 devices: a whole 4x4x8 slice. The times are simulated.
256 devices in a mesh: seq: 128 (over y_lo, z, x, core), ch: 2 (over y_hi).
Axes of the slice: x: 4, y: 4 (y_hi: 2, y_lo: 2; y = y_hi * 2 + y_lo), z: 8, core: 2. Of those that a mesh axis runs over, the one named last changes fastest.
Arguments:
- stream: bfloat16 [2, 8192, 1024], P(None, 'seq', 'ch'), may hold values from -6 to 6
- skip: bfloat16 [2, 32768, 512], P(None, 'seq', 'ch'), may hold values from -6 to 6
- norm_gain: float32 [2, 1024], replicated, may hold values from 0.1 to 1.9
- norm_shift: float32 [2, 1024], replicated, may hold values from -3 to 3
- conv_weight: bfloat16 [2, 3, 1024, 512], P(None, None, None, 'ch'), may hold values from -0.109375 to 0.109375
- mid_gain: float32 [2, 512], P(None, 'ch'), may hold values from 0.1 to 1.9
- mid_shift: float32 [2, 512], P(None, 'ch'), may hold values from -3 to 3
- mix_weight: bfloat16 [2, 512, 1024], P(None, 'ch'), may hold values from -0.25 to 0.25
- up_gain: float32 [1024], replicated, may hold values from 0.1 to 1.9
- up_shift: float32 [1024], replicated, may hold values from -3 to 3
- up_weight: bfloat16 [8, 1024, 512], P(None, None, 'ch'), may hold values from -0.125 to 0.125
Outputs:
- upsampled: bfloat16 [2, 32768, 512], P(None, 'seq', 'ch')
All inputs are finite; a program needn't handle non-finite values.
Results may differ from a plain program's by a relative error of at most 0.019.
Values may be sent and summed in bfloat16 or wider, within the bound.
A program may use at most 64 MiB of HBM per device.

v0:
```python
import jax
import jax.numpy as jnp
from jax import lax
from jax.sharding import PartitionSpec as P

RESIDUAL_LAYERS = 2


def with_halo(x, sides, width):
    for axis, dim in sides:
        devices, length = (lax.axis_size(axis), x.shape[dim])
        up = [(i, (i + 1) % devices) for i in range(devices - 1)]
        down = [(j, i) for i, j in up]
        last = lax.slice_in_dim(x, length - width, length, axis=dim)
        first = lax.slice_in_dim(x, 0, width, axis=dim)
        before = lax.ppermute(last, axis, up)
        after = lax.ppermute(first, axis, down)
        x = jnp.concatenate([before, x, after], axis=dim)
    return x


def gelu_act(values):
    return jax.nn.gelu(values)


def spread_taps(field, tap_spacing):
    return with_halo(field, (("seq", 1),), tap_spacing)


def body(
    stream,
    skip,
    norm_gain,
    norm_shift,
    conv_weight,
    mid_gain,
    mid_shift,
    mix_weight,
    up_gain,
    up_shift,
    up_weight,
):
    seq_count, shard_rows, local_width = stream.shape
    part_count = lax.axis_size("ch")
    own_index = lax.axis_index("ch")
    channels = local_width * part_count

    def local_slice(feature_vector):
        return lax.dynamic_slice_in_dim(feature_vector, own_index * local_width, local_width, 0)

    stream_now = stream
    for layer_number in range(RESIDUAL_LAYERS):
        tap_spacing = shard_rows // 2 ** (RESIDUAL_LAYERS - 1 - layer_number)
        activated = gelu_act(
            stream_now.astype(jnp.float32) * local_slice(norm_gain[layer_number])
            + local_slice(norm_shift[layer_number])
        ).astype(jnp.bfloat16)
        padded = spread_taps(lax.all_gather(activated, "ch", axis=2, tiled=True), tap_spacing)
        conv_out = jnp.zeros((seq_count * shard_rows, conv_weight.shape[3]), jnp.float32)
        for tap_index in range(3):
            receptive_span = padded[
                :, tap_index * tap_spacing : tap_index * tap_spacing + shard_rows
            ].reshape(-1, channels)
            conv_out = conv_out + jnp.dot(
                receptive_span,
                conv_weight[layer_number, tap_index],
                preferred_element_type=jnp.float32,
            )
        hidden = gelu_act(conv_out * mid_gain[layer_number] + mid_shift[layer_number]).astype(
            jnp.bfloat16
        )
        contrib = jnp.dot(
            hidden, mix_weight[layer_number], preferred_element_type=jnp.float32
        ).reshape(seq_count, shard_rows, channels)
        residual_delta = lax.psum_scatter(
            contrib.astype(jnp.bfloat16), "ch", scatter_dimension=2, tiled=True
        ).astype(jnp.float32)
        stream_now = (stream_now.astype(jnp.float32) + residual_delta).astype(jnp.bfloat16)
    coarse_local = gelu_act(
        stream_now.astype(jnp.float32) * local_slice(up_gain) + local_slice(up_shift)
    ).astype(jnp.bfloat16)
    gathered = lax.all_gather(coarse_local, "ch", axis=2, tiled=True)
    edged_rows = with_halo(gathered, (("seq", 1),), 1)
    projected = jnp.einsum(
        "blc,kcs->blks", edged_rows, up_weight, preferred_element_type=jnp.float32
    )
    centre = projected[:, 1 : shard_rows + 1, 2:6]
    from_prev = projected[:, 0:shard_rows, 6:8]
    from_next = projected[:, 2 : shard_rows + 2, 0:2]
    out_local = skip.shape[2]
    combined = (
        centre
        + jnp.concatenate([from_prev, from_next], axis=2)
        + skip.reshape(seq_count, shard_rows, 4, out_local).astype(jnp.float32)
    )
    return combined.reshape(seq_count, 4 * shard_rows, out_local).astype(jnp.bfloat16)


def solution(mesh):
    placed = (
        P(None, "seq", "ch"),
        P(None, "seq", "ch"),
        P(),
        P(),
        P(None, None, None, "ch"),
        P(None, "ch"),
        P(None, "ch"),
        P(None, "ch", None),
        P(),
        P(),
        P(None, None, "ch"),
    )
    return jax.shard_map(
        body, mesh=mesh, in_specs=placed, out_specs=P(None, "seq", "ch"), check_vma=False
    )
```

profile of v0, /device:TPU:8, one launch (start us, length us, event | category | flops | bytes accessed | tf_op | source)
XLA Modules:
  0.0 120.6 jit_solution(5190303392674618179)
XLA Ops:
  6.5 0.0 reduce-scatter.3.cloned.1.call-start
  6.5 0.9 fusion.90
  7.4 0.8 fusion.91
  8.2 0.0 copy-start.2
  8.3 1.1 fusion.37
  9.4 0.0 copy-start.1
  9.4 7.5 %all_gather.9 = bf16[2,64,1024]{2,1,0:T(8,128)(2,1)S(1)} all-gather(bf16[2,64,512]{2,1,0:T(8,128)(2,1)S(1)} %fusion.37), channel_id=1, replica_groups=mesh['seq'=128,'ch'=2] {'ch'}, dimensions={2}, use_global_device_ids=true | all-gather | bytes 393216 | tf_op jit(solution)/shard_map/all_gather | solution.py:58
  17.0 1.9 %collective-permute-start = (bf16[2,32,1024]{2,1,0:T(8,128)(2,1)S(1)}, bf16[2,32,1024]{2,1,0:T(8,128)(2,1)S(1)}, u32[]{:S(2)}, u32[]{:S(2)}) collective-permute-start(bf16[2,32,1024]{2,1,0:T(8,128)(2,1)S(1)} %get-tuple-element.11), channel_id=1, source_target_pairs={{0,2},{2,4},{4,6},{6,8},{8,10},{10,12},{12,14},{14,16},{16,18},{18... | collective-permute-start | bytes 393224 | tf_op jit(solution)/shard_map/ppermute | solution.py:16
  18.9 8.4 %collective-permute-start.1 = (bf16[2,32,1024]{2,1,0:T(8,128)(2,1)S(1)}, bf16[2,32,1024]{2,1,0:T(8,128)(2,1)S(1)}, u32[]{:S(2)}, u32[]{:S(2)}) collective-permute-start(bf16[2,32,1024]{2,1,0:T(8,128)(2,1)S(1)} %get-tuple-element.12), channel_id=1, source_target_pairs={{2,0},{4,2},{6,4},{8,6},{10,8},{12,10},{14,12},{16,14},{18,16},{20... | collective-permute-start | bytes 393224 | tf_op jit(solution)/shard_map/ppermute | solution.py:17
  27.3 0.8 fusion.92
  28.1 1.3 %fusion.19 = f32[128,256]{1,0:T(8,128)S(1)} fusion(bf16[128,1024]{1,0:T(8,128)(2,1)S(1)} %bitcast.68, bf16[2,3,1024,256]{3,2,1,0:T(8,128)(2,1)} %param.15), kind=kOutput, calls=%fused_computation.24 | convolution fusion | flops 67108864 | bytes 917504 | tf_op jit(solution)/shard_map/dot_general | solution.py:64
  29.4 0.8 fusion.93
  30.1 0.0 collective-permute-done
  30.1 0.0 collective-permute-done.1
  30.2 0.0 copy-done
  30.2 0.2 fusion.17
  30.4 0.3 fusion.71
  30.7 0.0 copy-start.5
  30.7 0.0 copy-start.6
  30.7 0.9 convolution_convert_fusion.1
  31.7 0.0 reduce-scatter.3.cloned.1.call-update
  31.7 0.0 reduce-scatter.5.cloned.1.call-start
  31.8 18.7 %reduce-scatter.3.cloned.1.call-done = bf16[2,64,512]{2,1,0:T(8,128)(2,1)} async-done(((bf16[2,64,1024]{2,1,0:T(8,128)(2,1)}), bf16[2,64,512]{2,1,0:T(8,128)(2,1)}) %reduce-scatter.3.cloned.1.call-update) | async-done | bytes 131088 | tf_op jit(solution)/shard_map/reduce_scatter | solution.py:75
  50.5 1.1 fusion.46
  51.6 7.4 %all_gather.10 = bf16[2,64,1024]{2,1,0:T(8,128)(2,1)S(1)} all-gather(bf16[2,64,512]{2,1,0:T(8,128)(2,1)S(1)} %fusion.46), channel_id=1, replica_groups=mesh['seq'=128,'ch'=2] {'ch'}, dimensions={2}, use_global_device_ids=true | all-gather | bytes 393216 | tf_op jit(solution)/shard_map/all_gather | solution.py:58
  59.0 6.8 %collective-permute-start.3 = (bf16[2,64,1024]{2,1,0:T(8,128)(2,1)S(1)}, bf16[2,64,1024]{2,1,0:T(8,128)(2,1)S(1)}, u32[]{:S(2)}, u32[]{:S(2)}) collective-permute-start(bf16[2,64,1024]{2,1,0:T(8,128)(2,1)S(1)} %all_gather.10), channel_id=1, source_target_pairs={{2,0},{4,2},{6,4},{8,6},{10,8},{12,10},{14,12},{16,14},{18,16},{20... | collective-permute-start | bytes 786440 | tf_op jit(solution)/shard_map/ppermute | solution.py:17
  65.8 1.9 %collective-permute-start.2 = (bf16[2,64,1024]{2,1,0:T(8,128)(2,1)S(1)}, bf16[2,64,1024]{2,1,0:T(8,128)(2,1)S(1)}, u32[]{:S(2)}, u32[]{:S(2)}) collective-permute-start(bf16[2,64,1024]{2,1,0:T(8,128)(2,1)S(1)} %all_gather.10), channel_id=1, source_target_pairs={{0,2},{2,4},{4,6},{6,8},{8,10},{10,12},{12,14},{14,16},{16,18},{18... | collective-permute-start | bytes 786440 | tf_op jit(solution)/shard_map/ppermute | solution.py:16
  67.7 0.2 fusion.13
  67.9 1.7 %collective-permute-done.3 = bf16[2,64,1024]{2,1,0:T(8,128)(2,1)S(1)} collective-permute-done((bf16[2,64,1024]{2,1,0:T(8,128)(2,1)S(1)}, bf16[2,64,1024]{2,1,0:T(8,128)(2,1)S(1)}, u32[]{:S(2)}, u32[]{:S(2)}) %collective-permute-start.3) | collective-permute-done | bytes 262176 | tf_op jit(solution)/shard_map/ppermute | solution.py:17
  69.7 0.2 fusion.11
  69.9 7.8 %collective-permute-done.2 = bf16[2,64,1024]{2,1,0:T(8,128)(2,1)S(1)} collective-permute-done((bf16[2,64,1024]{2,1,0:T(8,128)(2,1)S(1)}, bf16[2,64,1024]{2,1,0:T(8,128)(2,1)S(1)}, u32[]{:S(2)}, u32[]{:S(2)}) %collective-permute-start.2) | collective-permute-done | bytes 262176 | tf_op jit(solution)/shard_map/ppermute | solution.py:16
  77.7 0.3 fusion.83
  78.0 0.9 convolution_convert_fusion
  78.9 0.0 reduce-scatter.5.cloned.1.call-update
  79.0 0.1 dynamic_slice.22
  79.0 0.1 dynamic_slice.23
  79.1 10.7 %reduce-scatter.5.cloned.1.call-done = bf16[2,64,512]{2,1,0:T(8,128)(2,1)} async-done(((bf16[2,64,1024]{2,1,0:T(8,128)(2,1)}), bf16[2,64,512]{2,1,0:T(8,128)(2,1)}) %reduce-scatter.5.cloned.1.call-update) | async-done | bytes 131088 | tf_op jit(solution)/shard_map/reduce_scatter | solution.py:75
  89.8 1.1 fusion.61
  90.9 7.4 %all_gather.11 = bf16[2,64,1024]{2,1,0:T(8,128)(2,1)S(1)} all-gather(bf16[2,64,512]{2,1,0:T(8,128)(2,1)S(1)} %fusion.61), channel_id=1, replica_groups=mesh['seq'=128,'ch'=2] {'ch'}, dimensions={2}, use_global_device_ids=true | all-gather | bytes 393216 | tf_op jit(solution)/shard_map/all_gather | solution.py:82
  98.3 1.9 %collective-permute-start.4 = (bf16[2,1,1024]{2,1,0:T(2,128)(2,1)S(1)}, bf16[2,1,1024]{2,1,0:T(2,128)(2,1)S(1)}, u32[]{:S(2)}, u32[]{:S(2)}) collective-permute-start(bf16[2,1,1024]{2,1,0:T(2,128)(2,1)S(1)} %get-tuple-element.7), channel_id=1, source_target_pairs={{0,2},{2,4},{4,6},{6,8},{8,10},{10,12},{12,14},{14,16},{16,18},{18... | collective-permute-start | bytes 12296 | tf_op jit(solution)/shard_map/ppermute | solution.py:16
  100.2 7.9 %collective-permute-start.5 = (bf16[2,1,1024]{2,1,0:T(2,128)(2,1)S(1)}, bf16[2,1,1024]{2,1,0:T(2,128)(2,1)S(1)}, u32[]{:S(2)}, u32[]{:S(2)}) collective-permute-start(bf16[2,1,1024]{2,1,0:T(2,128)(2,1)S(1)} %get-tuple-element.8), channel_id=1, source_target_pairs={{2,0},{4,2},{6,4},{8,6},{10,8},{12,10},{14,12},{16,14},{18,16},{20... | collective-permute-start | bytes 12296 | tf_op jit(solution)/shard_map/ppermute | solution.py:17
  108.1 1.2 %copy.12 = f32[2,256,256]{2,0,1:T(2,128)S(1)} copy(bf16[2,256,256]{2,1,0:T(8,128)(2,1)} %param.12) | data formatting | bytes 786432 | tf_op jit(solution)/shard_map/convert_element_type | solution.py:94
  109.3 0.0 collective-permute-done.4
  109.3 0.1 collective-permute-done.5
  109.4 3.0 %fusion = f32[2,66,8,256]{3,1,2,0:T(8,128)S(1)} fusion(bf16[8,1024,256]{2,1,0:T(8,128)(2,1)} %param.21, bf16[2,1,1024]{2,1,0:T(2,128)(2,1)S(1)} %collective-permute-done.5, bf16[2,64,1024]{2,1,0:T(8,128)(2,1)S(1)} %all_gather.11, bf16[2,1,1024]{2,1,0:T(2,128)(2,1)S(1)} %collective-permute-done.4), kind=kOutput, calls=%fused_computation | convolution fusion | flops 554459136 | bytes 5545984 | tf_op jit(solution)/shard_map/blc,kcs->blks/dot_general | solution.py:84
  112.5 0.2 fusion.9
  112.7 0.3 copy.14
  113.0 0.7 copy.15
  (15 shorter events, 0.2 us)
Async XLA Ops:
  6.5 23.6 %copy-start = (bf16[2,3,1024,256]{3,2,1,0:T(8,128)(2,1)S(1)}, bf16[2,3,1024,256]{3,2,1,0:T(8,128)(2,1)}, u32[]{:S(2)}) copy-start(bf16[2,3,1024,256]{3,2,1,0:T(8,128)(2,1)} %param.15) | copy-start | bytes 9437188
  6.5 43.9 %reduce-scatter.3.cloned.1.call-start = ((), (), s32[]{:S(2)}) async-start(), calls=%async_computation.2 | async-start | bytes 393216 | tf_op jit(solution)/shard_map/reduce_scatter | solution.py:75
  8.2 22.5 %copy-start.2 = (bf16[2,256,1024]{2,1,0:T(8,128)(2,1)S(1)}, bf16[2,256,1024]{2,1,0:T(8,128)(2,1)}, u32[]{:S(2)}) copy-start(bf16[2,256,1024]{2,1,0:T(8,128)(2,1)} %param.18) | copy-start | bytes 3145732
  9.4 41.1 %copy-start.1 = (bf16[2,64,512]{2,1,0:T(8,128)(2,1)S(1)}, bf16[2,64,512]{2,1,0:T(8,128)(2,1)}, u32[]{:S(2)}) copy-start(bf16[2,64,512]{2,1,0:T(8,128)(2,1)} %param.11) | copy-start | bytes 393220
  17.0 13.2 %collective-permute-start = (bf16[2,32,1024]{2,1,0:T(8,128)(2,1)S(1)}, bf16[2,32,1024]{2,1,0:T(8,128)(2,1)S(1)}, u32[]{:S(2)}, u32[]{:S(2)}) collective-permute-start(bf16[2,32,1024]{2,1,0:T(8,128)(2,1)S(1)} %get-tuple-element.11), channel_id=1, source_target_pairs={{0,2},{2,4},{4,6},{6,8},{8,10},{10,12},{12,14},{14,16},{16,18},{18... | collective-permute-start | bytes 393224 | tf_op jit(solution)/shard_map/ppermute | solution.py:16
  18.9 11.2 %collective-permute-start.1 = (bf16[2,32,1024]{2,1,0:T(8,128)(2,1)S(1)}, bf16[2,32,1024]{2,1,0:T(8,128)(2,1)S(1)}, u32[]{:S(2)}, u32[]{:S(2)}) collective-permute-start(bf16[2,32,1024]{2,1,0:T(8,128)(2,1)S(1)} %get-tuple-element.12), channel_id=1, source_target_pairs={{2,0},{4,2},{6,4},{8,6},{10,8},{12,10},{14,12},{16,14},{18,16},{20... | collective-permute-start | bytes 393224 | tf_op jit(solution)/shard_map/ppermute | solution.py:17
  30.7 48.2 %copy-start.5 = (f32[1024]{0:T(1024)S(1)}, f32[1024]{0:T(1024)}, u32[]{:S(2)}) copy-start(f32[1024]{0:T(1024)} %param.19) | copy-start | bytes 12292
  30.7 48.3 %copy-start.6 = (f32[1024]{0:T(1024)S(1)}, f32[1024]{0:T(1024)}, u32[]{:S(2)}) copy-start(f32[1024]{0:T(1024)} %param.20) | copy-start | bytes 12292
  31.7 58.1 %reduce-scatter.5.cloned.1.call-start = ((), (), s32[]{:S(2)}) async-start(), calls=%async_computation.3 | async-start | bytes 393216 | tf_op jit(solution)/shard_map/reduce_scatter | solution.py:75
  50.5 27.5 %copy-start.3 = (bf16[2,256,1024]{2,1,0:T(8,128)(2,1)S(1)}, bf16[2,256,1024]{2,1,0:T(8,128)(2,1)}, u32[]{:S(2)}) copy-start(bf16[2,256,1024]{2,1,0:T(8,128)(2,1)} %param.18) | copy-start | bytes 3145732
  50.5 39.3 %copy-start.4 = (bf16[2,64,512]{2,1,0:T(8,128)(2,1)S(1)}, bf16[2,64,512]{2,1,0:T(8,128)(2,1)}, u32[]{:S(2)}) copy-start(bf16[2,64,512]{2,1,0:T(8,128)(2,1)} %reduce-scatter.3.cloned.1.call-done) | copy-start | bytes 393220
  59.0 10.7 %collective-permute-start.3 = (bf16[2,64,1024]{2,1,0:T(8,128)(2,1)S(1)}, bf16[2,64,1024]{2,1,0:T(8,128)(2,1)S(1)}, u32[]{:S(2)}, u32[]{:S(2)}) collective-permute-start(bf16[2,64,1024]{2,1,0:T(8,128)(2,1)S(1)} %all_gather.10), channel_id=1, source_target_pairs={{2,0},{4,2},{6,4},{8,6},{10,8},{12,10},{14,12},{16,14},{18,16},{20... | collective-permute-start | bytes 786440 | tf_op jit(solution)/shard_map/ppermute | solution.py:17
  65.8 11.9 %collective-permute-start.2 = (bf16[2,64,1024]{2,1,0:T(8,128)(2,1)S(1)}, bf16[2,64,1024]{2,1,0:T(8,128)(2,1)S(1)}, u32[]{:S(2)}, u32[]{:S(2)}) collective-permute-start(bf16[2,64,1024]{2,1,0:T(8,128)(2,1)S(1)} %all_gather.10), channel_id=1, source_target_pairs={{0,2},{2,4},{4,6},{6,8},{8,10},{10,12},{12,14},{14,16},{16,18},{18... | collective-permute-start | bytes 786440 | tf_op jit(solution)/shard_map/ppermute | solution.py:16
  98.3 11.0 %collective-permute-start.4 = (bf16[2,1,1024]{2,1,0:T(2,128)(2,1)S(1)}, bf16[2,1,1024]{2,1,0:T(2,128)(2,1)S(1)}, u32[]{:S(2)}, u32[]{:S(2)}) collective-permute-start(bf16[2,1,1024]{2,1,0:T(2,128)(2,1)S(1)} %get-tuple-element.7), channel_id=1, source_target_pairs={{0,2},{2,4},{4,6},{6,8},{8,10},{10,12},{12,14},{14,16},{16,18},{18... | collective-permute-start | bytes 12296 | tf_op jit(solution)/shard_map/ppermute | solution.py:16
  100.2 9.2 %collective-permute-start.5 = (bf16[2,1,1024]{2,1,0:T(2,128)(2,1)S(1)}, bf16[2,1,1024]{2,1,0:T(2,128)(2,1)S(1)}, u32[]{:S(2)}, u32[]{:S(2)}) collective-permute-start(bf16[2,1,1024]{2,1,0:T(2,128)(2,1)S(1)} %get-tuple-element.8), channel_id=1, source_target_pairs={{2,0},{4,2},{6,4},{8,6},{10,8},{12,10},{14,12},{16,14},{18,16},{20... | collective-permute-start | bytes 12296 | tf_op jit(solution)/shard_map/ppermute | solution.py:17
Sparse Core Ops, SparseCore 0:
  31.8 18.5 reduce-scatter.2
  79.1 10.6 reduce-scatter.4
where the time goes:
time: 123 us; the launch traced here: 121 us
  waiting for transfers between devices  39 us (32%)
  starting transfers between devices  28.9 us (23%)
  blocking collectives  22.4 us (18%)
  between operations  13.6 us (11%)
  matrix products  7.37 us (6%)
  local copies, waits for them, and re-layouts  5.73 us (5%)
  other arithmetic  3.55 us (3%)
    reduce_scatter x2, waiting for transfers between devices, body(): lax.psum_scatter(contrib.astype(jnp.bfloat16), 'ch', scatter_dimension=2,...  29.4 us
    ppermute x3, starting transfers between devices, with_halo(): after = lax.ppermute(first, axis, down)  23.1 us
    all_gather x2, blocking collectives, body(): lax.all_gather(activated, 'ch', axis=2, tiled=True)  14.9 us
    ppermute x3, waiting for transfers between devices, with_halo(): before = lax.ppermute(last, axis, up)  7.81 us
    all_gather x1, blocking collectives, body(): gathered = lax.all_gather(coarse_local, 'ch', axis=2, tiled=True)  7.43 us
    ppermute x3, starting transfers between devices, with_halo(): before = lax.ppermute(last, axis, up)  5.76 us
    dot_general x1, matrix products, body(): jnp.einsum('blc,kcs->blks', edged_rows, up_weight, preferred_element_type...  2.97 us
    dot_general x6, matrix products, body(): jnp.dot(receptive_span, conv_weight[layer_number, tap_index], preferred_e...  2.52 us
  transfers between devices with their start and end apart: 8, of which 5 were waited for; matrix products, arithmetic and copies ran while one was open for 4% of the time, Pallas kernels for 0%

commit v1 on v0

v1 whole, which is shorter than its diff:
```python
import functools

import jax
import jax.numpy as jnp
from jax import lax
from jax.experimental import pallas as pl
from jax.experimental.pallas import tpu as pltpu
from jax.sharding import PartitionSpec as P

MESH = pl.DeviceIdType.MESH
F32 = jnp.float32
BF16 = jnp.bfloat16
ROWS = 64
GELU_A = 0.7978845608028654
GELU_B = 0.7978845608028654 * 0.044715


def gelu(v):
    half = 0.5 * v
    return half + half * jnp.tanh(v * (GELU_A + GELU_B * (v * v)))


def dot(a, b):
    return jnp.dot(a, b, preferred_element_type=F32)


def kernel(
    seq_devices,
    stream, skip, norm_gain, norm_shift, conv_weight, mid_gain, mid_shift, mix_weight, up_gain, up_shift, up_weight,
    out,
    xr, a0, hb, mw, cw, uw, a1, x1, h1, eh, uf, outf, outb, skipb, ng, ns, mg, ms, ug, us,
    local_sem, send_sem, recv_sem,
):
    s = lax.axis_index("seq")
    g = lax.axis_index("ch")
    core = lax.rem(s, 2)
    o = 1 - g
    sib_s = s + 1 - 2 * core
    crs_s = lax.rem(s + seq_devices - 1 + 2 * core, seq_devices)
    cut_s = lax.rem(s + seq_devices // 2, seq_devices)
    par = {"seq": s, "ch": o}
    sib = {"seq": sib_s, "ch": g}
    crs = {"seq": crs_s, "ch": g}
    dcr = {"seq": crs_s, "ch": o}
    dsb = {"seq": sib_s, "ch": o}
    cut = {"seq": cut_s, "ch": o}
    partners = (par, sib, crs, dcr, dsb, cut)

    barrier = pltpu.get_barrier_semaphore()
    for device in partners:
        pl.semaphore_signal(barrier, inc=1, device_id=device, device_id_type=MESH)

    local = []

    def fetch(src, dst):
        copy = pltpu.make_async_copy(src, dst, local_sem.at[len(local)])
        copy.start()
        local.append(copy)
        return copy

    own_copy = fetch(stream, xr.at[g, 1])
    gain_copies = [
        fetch(norm_gain, ng), fetch(norm_shift, ns), fetch(mid_gain, mg), fetch(mid_shift, ms),
    ]
    cw0_copy = fetch(conv_weight.at[0], cw.at[0])
    mw0_copy = fetch(mix_weight.at[0], mw.at[0, g])
    cw1_copy = fetch(conv_weight.at[1], cw.at[1])
    mw1_copy = fetch(mix_weight.at[1], mw.at[1, g])
    up_copies = [fetch(up_gain, ug), fetch(up_shift, us), fetch(up_weight, uw), fetch(skip, skipb)]

    sends = []

    def send(src, dst, device):
        index = len(sends)
        copy = pltpu.make_async_remote_copy(
            src_ref=src, dst_ref=dst, send_sem=send_sem.at[index], recv_sem=recv_sem.at[index],
            device_id=device, device_id_type=MESH,
        )
        copy.start()
        sends.append(copy)
        return copy

    to_sib = 2 * core
    to_crs = 2 - 2 * core
    my_sib = 2 - 2 * core
    my_crs = 2 * core
    near = pl.ds(pl.multiple_of(32 * core, 32), 32)
    far = pl.ds(pl.multiple_of(32 - 32 * core, 32), 32)

    pl.semaphore_wait(barrier, len(partners))
    x_par = send(stream, xr.at[g, 1], par)
    x_dcr = send(stream.at[:, near], xr.at[g, to_crs, :, near], dcr)
    x_crs = send(stream.at[:, near], xr.at[g, to_crs, :, near], crs)
    x_sib = send(stream, xr.at[g, to_sib], sib)
    x_dcr2 = send(stream.at[:, far], xr.at[g, to_crs, :, far], dcr)
    x_crs2 = send(stream.at[:, far], xr.at[g, to_crs, :, far], crs)
    mine = pl.ds(pl.multiple_of(128 * core, 128), 128)
    w_cut = [send(mix_weight.at[0, mine], mw.at[0, g, mine], cut)]

    crs_valid = jnp.where(jnp.logical_and(s > 0, s < seq_devices - 1), 1.0, 0.0).astype(F32)
    left_valid = jnp.where(s > 0, 1.0, 0.0).astype(F32)
    right_valid = jnp.where(s < seq_devices - 1, 1.0, 0.0).astype(F32)

    def activate0(gg, slot, rows, dst_row, valid):
        cols = pl.ds(pl.multiple_of(gg * 512, 512), 512)
        gain = ng[0:1, cols]
        shift = ns[0:1, cols]
        for b in range(2):
            v = gelu(xr[gg, slot, b, rows, :].astype(F32) * gain + shift)
            if valid is not None:
                v = v * valid
            a0[gg, b, dst_row, :] = v.astype(BF16)

    def conv0(gg):
        acc = None
        for k in range(3):
            term = dot(
                a0[gg, :, 32 * k : 32 * k + ROWS, :].reshape(128, 512),
                cw[0, k, pl.ds(pl.multiple_of(gg * 512, 512), 512), :],
            )
            acc = term if acc is None else acc + term
        return acc

    sib_src = pl.ds(pl.multiple_of(32 * core, 32), 32)
    crs_src = pl.ds(pl.multiple_of(32 - 32 * core, 32), 32)
    sib_dst = pl.ds(pl.multiple_of(96 - 96 * core, 32), 32)
    crs_dst = pl.ds(pl.multiple_of(96 * core, 32), 32)
    whole = pl.ds(0, ROWS)
    centre = pl.ds(32, ROWS)

    own_copy.wait()
    for copy in gain_copies:
        copy.wait()
    activate0(g, 1, whole, centre, None)
    x_sib.wait_recv()
    activate0(g, my_sib, sib_src, sib_dst, None)
    x_crs.wait_recv()
    activate0(g, my_crs, crs_src, crs_dst, crs_valid)
    cw0_copy.wait()
    acc = conv0(g)
    x_par.wait_recv()
    x_fwd = send(xr.at[o, 1], xr.at[o, to_sib], sib)
    activate0(o, 1, whole, centre, None)
    x_dcr.wait_recv()
    activate0(o, my_crs, crs_src, crs_dst, crs_valid)
    x_fwd.wait_recv()
    activate0(o, my_sib, sib_src, sib_dst, None)
    acc = acc + conv0(o)
    hb[g, 1] = gelu(acc * mg[0:1, :] + ms[0:1, :]).astype(BF16)

    h_par = send(hb.at[g, 1], hb.at[g, 1], par)
    h_dcr = send(hb.at[g, 1], hb.at[g, to_crs], dcr)
    h_crs = send(hb.at[g, 1], hb.at[g, to_crs], crs)
    h_sib = send(hb.at[g, 1], hb.at[g, to_sib], sib)
    w_cut.append(send(mix_weight.at[1, mine], mw.at[1, g, mine], cut))
    w_cut[0].wait_recv()
    w_fwd = [send(mw.at[0, o, mine], mw.at[0, o, mine], sib)]

    def mix0(slot, valid):
        for n in range(4):
            cols = slice(256 * n, 256 * n + 256)
            gg, inner = n // 2, slice(256 * (n % 2), 256 * (n % 2) + 256)
            z = dot(hb[0, slot], mw[0, 0, :, cols]) + dot(hb[1, slot], mw[0, 1, :, cols])
            x = xr[gg, slot, :, :, inner].reshape(128, 256).astype(F32) + z
            x = x.astype(BF16)
            x1[slot, :, cols] = x
            v = gelu(x.astype(F32) * ng[1:2, cols] + ns[1:2, cols])
            if valid is not None:
                v = v * valid
            a1[slot, :, cols] = v.astype(BF16)
        return dot(a1[slot], cw[1, slot])

    mw0_copy.wait()
    cw1_copy.wait()
    h_par.wait_recv()
    h_fwd = send(hb.at[o, 1], hb.at[o, to_sib], sib)
    w_fwd[0].wait_recv()
    acc = mix0(1, None)
    h_sib.wait_recv()
    h_fwd.wait_recv()
    acc = acc + mix0(my_sib, None)
    x_crs2.wait_recv()
    x_dcr2.wait_recv()
    h_crs.wait_recv()
    h_dcr.wait_recv()
    acc = acc + mix0(my_crs, crs_valid)
    h1[g] = gelu(acc * mg[1:2, :] + ms[1:2, :]).astype(BF16).reshape(2, ROWS, 256)

    last = pl.ds(pl.multiple_of(48 - 48 * core, 16), 16)
    first = pl.ds(pl.multiple_of(48 * core, 16), 16)
    g_par = send(h1.at[g], h1.at[g], par)
    g_dcr = send(h1.at[g, :, first], eh.at[g, 1 - core], dcr)
    g_crs = send(h1.at[g, :, first], eh.at[g, 1 - core], crs)
    g_dsb = send(h1.at[g, :, last], eh.at[g, core], dsb)
    g_sib = send(h1.at[g, :, last], eh.at[g, core], sib)

    w_cut[1].wait_recv()
    w_fwd.append(send(mw.at[1, o, mine], mw.at[1, o, mine], sib))
    mw1_copy.wait()
    for copy in up_copies:
        copy.wait()
    w_fwd[1].wait_recv()

    def top(h_pair, base, cols):
        z = dot(h_pair[0], mw[1, 0, :, cols]) + dot(h_pair[1], mw[1, 1, :, cols])
        x = (base.astype(F32) + z).astype(BF16).astype(F32)
        v = gelu(x * ug[0:1, cols] + us[0:1, cols])
        return v.astype(BF16).astype(F32)

    g_par.wait_recv()
    for n in range(4):
        cols = slice(256 * n, 256 * n + 256)
        u = top([h1[0].reshape(128, 256), h1[1].reshape(128, 256)], x1[1, :, cols], cols)
        for b in range(2):
            uf[b, 8 : 8 + ROWS, cols] = u[ROWS * b : ROWS * b + ROWS]
    for copy in (g_sib, g_crs, g_dsb, g_dcr):
        copy.wait_recv()
    for n in range(4):
        cols = slice(256 * n, 256 * n + 256)
        for side in range(2):
            first_row = 48 if side == 0 else 0
            base = jnp.concatenate(
                [x1[2 * side, ROWS * b + first_row : ROWS * b + first_row + 16, cols] for b in range(2)], axis=0
            )
            u = top([eh[0, side].reshape(32, 256), eh[1, side].reshape(32, 256)], base, cols)
            u = u * (left_valid if side == 0 else right_valid)
            for b in range(2):
                if side == 0:
                    uf[b, 0:8, cols] = u[16 * b + 8 : 16 * b + 16]
                else:
                    uf[b, 8 + ROWS : 16 + ROWS, cols] = u[16 * b : 16 * b + 8]

    def rows_at(offset):
        return jnp.concatenate(
            [uf[b, 8 + offset : 8 + offset + ROWS, :].astype(BF16) for b in range(2)], axis=0
        )

    here, before, after = rows_at(0), rows_at(-1), rows_at(1)
    for r in range(4):
        if r < 2:
            v = dot(here, uw[2 + r]) + dot(before, uw[6 + r])
        else:
            v = dot(here, uw[2 + r]) + dot(after, uw[r - 2])
        for b in range(2):
            for half in range(2):
                outf[b, half, pl.ds(r, ROWS, stride=4), :] = v[
                    ROWS * b : ROWS * b + ROWS, 128 * half : 128 * half + 128
                ]
    for half in range(2):
        lanes = slice(128 * half, 128 * half + 128)
        outb[:, :, lanes] = (outf[:, half] + skipb[:, :, lanes].astype(F32)).astype(BF16)
    out_copy = pltpu.make_async_copy(outb, out, local_sem.at[len(local)])
    out_copy.start()
    for copy in sends:
        copy.wait_send()
    out_copy.wait()


def body(
    seq_devices, stream, skip, norm_gain, norm_shift, conv_weight, mid_gain, mid_shift, mix_weight, up_gain, up_shift, up_weight
):
    anywhere = pl.BlockSpec(memory_space=pl.ANY)
    return pl.pallas_call(
        functools.partial(kernel, seq_devices),
        name="bottleneck",
        out_shape=jax.ShapeDtypeStruct((2, 256, 256), BF16),
        in_specs=[anywhere] * 11,
        out_specs=anywhere,
        scratch_shapes=[
            pltpu.VMEM((2, 3, 2, 64, 512), BF16),
            pltpu.VMEM((2, 2, 128, 512), BF16),
            pltpu.VMEM((2, 3, 128, 256), BF16),
            pltpu.VMEM((2, 2, 256, 1024), BF16),
            pltpu.VMEM((2, 3, 1024, 256), BF16),
            pltpu.VMEM((8, 1024, 256), BF16),
            pltpu.VMEM((3, 128, 1024), BF16),
            pltpu.VMEM((3, 128, 1024), BF16),
            pltpu.VMEM((2, 2, 64, 256), BF16),
            pltpu.VMEM((2, 2, 2, 16, 256), BF16),
            pltpu.VMEM((2, 80, 1024), F32),
            pltpu.VMEM((2, 2, 256, 128), F32),
            pltpu.VMEM((2, 256, 256), BF16),
            pltpu.VMEM((2, 256, 256), BF16),
            pltpu.VMEM((2, 1024), F32),
            pltpu.VMEM((2, 1024), F32),
            pltpu.VMEM((2, 256), F32),
            pltpu.VMEM((2, 256), F32),
            pltpu.VMEM((1, 1024), F32),
            pltpu.VMEM((1, 1024), F32),
            pltpu.SemaphoreType.DMA((16,)),
            pltpu.SemaphoreType.DMA((24,)),
            pltpu.SemaphoreType.DMA((24,)),
        ],
        compiler_params=pltpu.CompilerParams(
            collective_id=0, has_side_effects=True, vmem_limit_bytes=63 * 1024 * 1024
        ),
    )(
        stream, skip, norm_gain, norm_shift, conv_weight, mid_gain, mid_shift, mix_weight,
        up_gain.reshape(1, -1), up_shift.reshape(1, -1), up_weight,
    )


def solution(mesh):
    placed = (
        P(None, "seq", "ch"),
        P(None, "seq", "ch"),
        P(),
        P(),
        P(None, None, None, "ch"),
        P(None, "ch"),
        P(None, "ch"),
        P(None, "ch", None),
        P(),
        P(),
        P(None, None, "ch"),
    )
    return jax.shard_map(
        functools.partial(body, mesh.shape["seq"]),
        mesh=mesh, in_specs=placed, out_specs=P(None, "seq", "ch"), check_vma=False,
    )
```

time: 123 us -> 36.4 us (0.30); the launches traced: 121 us -> 36 us
  waiting for transfers between devices: 39 us -> 0 us
  Pallas kernels: 0 us -> 34.3 us
  starting transfers between devices: 28.9 us -> 0 us
  blocking collectives: 22.4 us -> 0 us
  between operations: 13.6 us -> 0.01 us
  matrix products: 7.37 us -> 0 us
  local copies, waits for them, and re-layouts: 5.73 us -> 1.67 us
  other arithmetic: 3.55 us -> 0 us
    pallas_call x0 -> x1, Pallas kernels: none -> 34.3 us  [body(): pl.pallas_call(functools.partial(kernel, seq_devices), name='bottleneck',...]
    reduce_scatter x2 -> x0, waiting for transfers between devices: 29.4 us -> none  [body(): lax.psum_scatter(contrib.astype(jnp.bfloat16), 'ch', scatter_dimension=2,...]
    ppermute x6 -> x0, starting transfers between devices: 28.8 us -> none  [the longest x3 23.1 us: with_halo(): after = lax.ppermute(first, axis, down)]
    all_gather x3 -> x0, blocking collectives: 22.4 us -> none  [the longest x2 14.9 us: body(): lax.all_gather(activated, 'ch', axis=2, tiled=True)]
    ppermute x6 -> x0, waiting for transfers between devices: 9.62 us -> none  [the longest x3 7.81 us: with_halo(): before = lax.ppermute(last, axis, up)]
    dot_general x9 -> x0, matrix products: 7.37 us -> none  [the longest x1 2.97 us: body(): jnp.einsum('blc,kcs->blks', edged_rows, up_weight, preferred_element_type...]
    convert_element_type x4 -> x0, other arithmetic: 3.51 us -> none  [the longest x2 2.24 us: body(): activated = gelu_act(stream_now.astype(jnp.float32) * local_slice(norm_ga...]
    slice x7 -> x0, local copies, waits for them, and re-layouts: 3.29 us -> none  [the longest x1 0.87 us: body(): norm_gain[layer_number]]
  transfers between devices with their start and end apart: 8 -> 0, of which waited for: 5 -> 0; matrix products, arithmetic and copies ran while one was open for 4% -> 0% of each run, Pallas kernels for 0% -> 0%
where the time goes in v1:
time: 36.4 us; the launch traced here: 36 us
  Pallas kernels  34.3 us (94%)
  local copies, waits for them, and re-layouts  1.67 us (5%)
    pallas_call x1, Pallas kernels, body(): pl.pallas_call(functools.partial(kernel, seq_devices), name='bottleneck',...  34.3 us
    unnamed x1, local copies, waits for them, and re-layouts  1.67 us

profile of v1, /device:TPU:8, one launch (start us, length us, event | category | flops | bytes accessed | tf_op | source)
XLA Modules:
  0.0 36.0 jit_solution(14253841230463905305)
XLA Ops:
  0.0 34.3 %bottleneck.1 = bf16[2,256,256]{2,1,0:T(8,128)(2,1)} custom-call(bf16[2,64,512]{2,1,0:T(8,128)(2,1)} %stream.1, bf16[2,256,256]{2,1,0:T(8,128)(2,1)} %skip.1, f32[2,1024]{1,0:T(2,128)} %norm_gain.1, f32[2,1024]{1,0:T(2,128)} %norm_shift.1, bf16[2,3,1024,256]{3,2,1,0:T(8,128)(2,1)} %conv_weight.1, f32[2,256]{1,0:T(2,128)} %mid_gain.1, f32[2,256]{1,0:T(2,128)} %mid_shift.1, ...), custom_call_target="tpu_custom_call" | custom-call | tf_op jit(solution)/shard_map/bottleneck/pallas_call | solution.py:263
  34.3 1.7 %copy.13 = bf16[2,256,256]{2,1,0:T(8,128)(2,1)} copy(bf16[2,256,256]{2,1,0:T(8,128)(2,1)} %bottleneck.1) | data formatting | bytes 524288

commit v2 on v1

--- a/solution.py
+++ b/solution.py
@@ -28,7 +28,7 @@
     seq_devices,
     stream, skip, norm_gain, norm_shift, conv_weight, mid_gain, mid_shift, mix_weight, up_gain, up_shift, up_weight,
     out,
-    xr, a0, hb, mw, cw, uw, a1, x1, h1, eh, uf, outf, outb, skipb, ng, ns, mg, ms, ug, us,
+    xr, a0, hb, mw, cw, uw, a1, x1, h1, eh, uf, outf, skipb, ng, ns, mg, ms, ug, us,
     local_sem, send_sem, recv_sem,
 ):
     s = lax.axis_index("seq")
@@ -38,17 +38,28 @@
     sib_s = s + 1 - 2 * core
     crs_s = lax.rem(s + seq_devices - 1 + 2 * core, seq_devices)
     cut_s = lax.rem(s + seq_devices // 2, seq_devices)
+    x_bit = lax.rem(s // 2, 2)
+    z_bit = lax.rem(s // 8, 2)
+    x_step = 2 - 4 * x_bit
+    z_step = 8 - 16 * z_bit
+    has_crs = jnp.logical_and(s > 0, s < seq_devices - 1)
     par = {"seq": s, "ch": o}
     sib = {"seq": sib_s, "ch": g}
     crs = {"seq": crs_s, "ch": g}
     dcr = {"seq": crs_s, "ch": o}
     dsb = {"seq": sib_s, "ch": o}
     cut = {"seq": cut_s, "ch": o}
-    partners = (par, sib, crs, dcr, dsb, cut)
+    mates = [{"seq": s + x_step, "ch": g}, {"seq": s + z_step, "ch": g}, {"seq": s + x_step + z_step, "ch": g}]
+    partners = [par, sib, dsb, cut] + mates
 
     barrier = pltpu.get_barrier_semaphore()
     for device in partners:
         pl.semaphore_signal(barrier, inc=1, device_id=device, device_id_type=MESH)
+
+    @pl.when(has_crs)
+    def _():
+        for device in (crs, dcr):
+            pl.semaphore_signal(barrier, inc=1, device_id=device, device_id_type=MESH)
 
     local = []
 
@@ -70,15 +81,28 @@
 
     sends = []
 
-    def send(src, dst, device):
+    def send(src, dst, device, when=None):
         index = len(sends)
         copy = pltpu.make_async_remote_copy(
             src_ref=src, dst_ref=dst, send_sem=send_sem.at[index], recv_sem=recv_sem.at[index],
             device_id=device, device_id_type=MESH,
         )
-        copy.start()
-        sends.append(copy)
+        sends.append((copy, when))
+        if when is None:
+            copy.start()
+        else:
+            pl.when(when)(copy.start)
         return copy
+
+    def arrive(*copies):
+        for copy in copies:
+            copy.wait_recv()
+
+    def arrive_crs(*copies):
+        @pl.when(has_crs)
+        def _():
+            for copy in copies:
+                copy.wait_recv()
 
     to_sib = 2 * core
     to_crs = 2 - 2 * core
@@ -86,20 +110,19 @@
     my_crs = 2 * core
     near = pl.ds(pl.multiple_of(32 * core, 32), 32)
     far = pl.ds(pl.multiple_of(32 - 32 * core, 32), 32)
-
-    pl.semaphore_wait(barrier, len(partners))
-    x_par = send(stream, xr.at[g, 1], par)
-    x_dcr = send(stream.at[:, near], xr.at[g, to_crs, :, near], dcr)
-    x_crs = send(stream.at[:, near], xr.at[g, to_crs, :, near], crs)
-    x_sib = send(stream, xr.at[g, to_sib], sib)
-    x_dcr2 = send(stream.at[:, far], xr.at[g, to_crs, :, far], dcr)
-    x_crs2 = send(stream.at[:, far], xr.at[g, to_crs, :, far], crs)
     mine = pl.ds(pl.multiple_of(128 * core, 128), 128)
-    w_cut = [send(mix_weight.at[0, mine], mw.at[0, g, mine], cut)]
-
-    crs_valid = jnp.where(jnp.logical_and(s > 0, s < seq_devices - 1), 1.0, 0.0).astype(F32)
-    left_valid = jnp.where(s > 0, 1.0, 0.0).astype(F32)
-    right_valid = jnp.where(s < seq_devices - 1, 1.0, 0.0).astype(F32)
+    eighth = pl.ds(pl.multiple_of(128 * core + 64 * z_bit + 32 * x_bit, 32), 32)
+
+    own_copy.wait()
+    pl.semaphore_wait(barrier, jnp.where(has_crs, len(partners) + 2, len(partners)))
+    x_own = xr.at[g, 1]
+    x_par = send(x_own, xr.at[g, 1], par)
+    x_crs = send(xr.at[g, 1, :, near], xr.at[g, to_crs, :, near], crs, has_crs)
+    x_dcr = send(xr.at[g, 1, :, near], xr.at[g, to_crs, :, near], dcr, has_crs)
+    x_sib = send(x_own, xr.at[g, to_sib], sib)
+    w_cut = [send(mix_weight.at[n, eighth], mw.at[n, g, eighth], cut) for n in range(2)]
+    x_crs2 = send(xr.at[g, 1, :, far], xr.at[g, to_crs, :, far], crs, has_crs)
+
 
     def activate0(gg, slot, rows, dst_row, valid):
         cols = pl.ds(pl.multiple_of(gg * 512, 512), 512)
@@ -108,7 +131,7 @@
         for b in range(2):
             v = gelu(xr[gg, slot, b, rows, :].astype(F32) * gain + shift)
             if valid is not None:
-                v = v * valid
+                v = jnp.where(valid, v, 0.0)
             a0[gg, b, dst_row, :] = v.astype(BF16)
 
     def conv0(gg):
@@ -128,32 +151,36 @@
     whole = pl.ds(0, ROWS)
     centre = pl.ds(32, ROWS)
 
-    own_copy.wait()
     for copy in gain_copies:
         copy.wait()
     activate0(g, 1, whole, centre, None)
-    x_sib.wait_recv()
+    arrive(x_sib)
     activate0(g, my_sib, sib_src, sib_dst, None)
-    x_crs.wait_recv()
-    activate0(g, my_crs, crs_src, crs_dst, crs_valid)
+    arrive_crs(x_crs)
+    activate0(g, my_crs, crs_src, crs_dst, has_crs)
     cw0_copy.wait()
     acc = conv0(g)
-    x_par.wait_recv()
+    arrive(x_par)
     x_fwd = send(xr.at[o, 1], xr.at[o, to_sib], sib)
     activate0(o, 1, whole, centre, None)
-    x_dcr.wait_recv()
-    activate0(o, my_crs, crs_src, crs_dst, crs_valid)
-    x_fwd.wait_recv()
+    arrive_crs(x_dcr)
+    activate0(o, my_crs, crs_src, crs_dst, has_crs)
+    arrive(w_cut[0])
+    w_mate = [[send(mw.at[0, o, eighth], mw.at[0, o, eighth], mate) for mate in mates]]
+    arrive(x_fwd)
     activate0(o, my_sib, sib_src, sib_dst, None)
     acc = acc + conv0(o)
     hb[g, 1] = gelu(acc * mg[0:1, :] + ms[0:1, :]).astype(BF16)
 
-    h_par = send(hb.at[g, 1], hb.at[g, 1], par)
-    h_dcr = send(hb.at[g, 1], hb.at[g, to_crs], dcr)
-    h_crs = send(hb.at[g, 1], hb.at[g, to_crs], crs)
-    h_sib = send(hb.at[g, 1], hb.at[g, to_sib], sib)
-    w_cut.append(send(mix_weight.at[1, mine], mw.at[1, g, mine], cut))
-    w_cut[0].wait_recv()
+    h_own = hb.at[g, 1]
+    h_par = send(h_own, hb.at[g, 1], par)
+    h_crs = send(h_own, hb.at[g, to_crs], crs, has_crs)
+    h_dcr = send(h_own, hb.at[g, to_crs], dcr, has_crs)
+    h_sib = send(h_own, hb.at[g, to_sib], sib)
+    x_rel = send(xr.at[o, 1, :, far], xr.at[o, to_crs, :, far], crs, has_crs)
+    arrive(w_cut[1])
+    w_mate.append([send(mw.at[1, o, eighth], mw.at[1, o, eighth], mate) for mate in mates])
+    arrive(*w_mate[0])
     w_fwd = [send(mw.at[0, o, mine], mw.at[0, o, mine], sib)]
 
     def mix0(slot, valid):
@@ -166,40 +193,40 @@
             x1[slot, :, cols] = x
             v = gelu(x.astype(F32) * ng[1:2, cols] + ns[1:2, cols])
             if valid is not None:
-                v = v * valid
+                v = jnp.where(valid, v, 0.0)
             a1[slot, :, cols] = v.astype(BF16)
         return dot(a1[slot], cw[1, slot])
 
     mw0_copy.wait()
     cw1_copy.wait()
-    h_par.wait_recv()
+    arrive(h_par)
     h_fwd = send(hb.at[o, 1], hb.at[o, to_sib], sib)
-    w_fwd[0].wait_recv()
+    arrive(w_fwd[0])
     acc = mix0(1, None)
-    h_sib.wait_recv()
-    h_fwd.wait_recv()
+    arrive(h_sib)
+    arrive(h_fwd)
     acc = acc + mix0(my_sib, None)
-    x_crs2.wait_recv()
-    x_dcr2.wait_recv()
-    h_crs.wait_recv()
-    h_dcr.wait_recv()
-    acc = acc + mix0(my_crs, crs_valid)
+    arrive_crs(x_crs2)
+    arrive_crs(x_rel)
+    arrive_crs(h_crs)
+    arrive_crs(h_dcr)
+    acc = acc + mix0(my_crs, has_crs)
     h1[g] = gelu(acc * mg[1:2, :] + ms[1:2, :]).astype(BF16).reshape(2, ROWS, 256)
 
     last = pl.ds(pl.multiple_of(48 - 48 * core, 16), 16)
     first = pl.ds(pl.multiple_of(48 * core, 16), 16)
     g_par = send(h1.at[g], h1.at[g], par)
-    g_dcr = send(h1.at[g, :, first], eh.at[g, 1 - core], dcr)
-    g_crs = send(h1.at[g, :, first], eh.at[g, 1 - core], crs)
+    g_crs = send(h1.at[g, :, first], eh.at[g, 1 - core], crs, has_crs)
+    g_dcr = send(h1.at[g, :, first], eh.at[g, 1 - core], dcr, has_crs)
     g_dsb = send(h1.at[g, :, last], eh.at[g, core], dsb)
     g_sib = send(h1.at[g, :, last], eh.at[g, core], sib)
 
-    w_cut[1].wait_recv()
+    arrive(*w_mate[1])
     w_fwd.append(send(mw.at[1, o, mine], mw.at[1, o, mine], sib))
     mw1_copy.wait()
     for copy in up_copies:
         copy.wait()
-    w_fwd[1].wait_recv()
+    arrive(w_fwd[1])
 
     def top(h_pair, base, cols):
         z = dot(h_pair[0], mw[1, 0, :, cols]) + dot(h_pair[1], mw[1, 1, :, cols])
@@ -207,14 +234,14 @@
         v = gelu(x * ug[0:1, cols] + us[0:1, cols])
         return v.astype(BF16).astype(F32)
 
-    g_par.wait_recv()
+    arrive(g_par)
     for n in range(4):
         cols = slice(256 * n, 256 * n + 256)
         u = top([h1[0].reshape(128, 256), h1[1].reshape(128, 256)], x1[1, :, cols], cols)
         for b in range(2):
             uf[b, 8 : 8 + ROWS, cols] = u[ROWS * b : ROWS * b + ROWS]
-    for copy in (g_sib, g_crs, g_dsb, g_dcr):
-        copy.wait_recv()
+    arrive(g_sib, g_dsb)
+    arrive_crs(g_crs, g_dcr)
     for n in range(4):
         cols = slice(256 * n, 256 * n + 256)
         for side in range(2):
@@ -223,7 +250,7 @@
                 [x1[2 * side, ROWS * b + first_row : ROWS * b + first_row + 16, cols] for b in range(2)], axis=0
             )
             u = top([eh[0, side].reshape(32, 256), eh[1, side].reshape(32, 256)], base, cols)
-            u = u * (left_valid if side == 0 else right_valid)
+            u = jnp.where(s > 0 if side == 0 else s < seq_devices - 1, u, 0.0)
             for b in range(2):
                 if side == 0:
                     uf[b, 0:8, cols] = u[16 * b + 8 : 16 * b + 16]
@@ -248,12 +275,12 @@
                 ]
     for half in range(2):
         lanes = slice(128 * half, 128 * half + 128)
-        outb[:, :, lanes] = (outf[:, half] + skipb[:, :, lanes].astype(F32)).astype(BF16)
-    out_copy = pltpu.make_async_copy(outb, out, local_sem.at[len(local)])
-    out_copy.start()
-    for copy in sends:
-        copy.wait_send()
-    out_copy.wait()
+        out[:, :, lanes] = (outf[:, half] + skipb[:, :, lanes].astype(F32)).astype(BF16)
+    for copy, when in sends:
+        if when is None:
+            copy.wait_send()
+        else:
+            pl.when(when)(copy.wait_send)
 
 
 def body(
@@ -263,9 +290,9 @@
     return pl.pallas_call(
         functools.partial(kernel, seq_devices),
         name="bottleneck",
-        out_shape=jax.ShapeDtypeStruct((2, 256, 256), BF16),
+        out_shape=pltpu.VMEM((2, 256, 256), BF16),
         in_specs=[anywhere] * 11,
-        out_specs=anywhere,
+        out_specs=pl.BlockSpec(memory_space=pltpu.VMEM),
         scratch_shapes=[
             pltpu.VMEM((2, 3, 2, 64, 512), BF16),
             pltpu.VMEM((2, 2, 128, 512), BF16),
@@ -280,7 +307,6 @@
             pltpu.VMEM((2, 80, 1024), F32),
             pltpu.VMEM((2, 2, 256, 128), F32),
             pltpu.VMEM((2, 256, 256), BF16),
-            pltpu.VMEM((2, 256, 256), BF16),
             pltpu.VMEM((2, 1024), F32),
             pltpu.VMEM((2, 1024), F32),
             pltpu.VMEM((2, 256), F32),
@@ -288,11 +314,11 @@
             pltpu.VMEM((1, 1024), F32),
             pltpu.VMEM((1, 1024), F32),
             pltpu.SemaphoreType.DMA((16,)),
-            pltpu.SemaphoreType.DMA((24,)),
-            pltpu.SemaphoreType.DMA((24,)),
+            pltpu.SemaphoreType.DMA((32,)),
+            pltpu.SemaphoreType.DMA((32,)),
         ],
         compiler_params=pltpu.CompilerParams(
-            collective_id=0, has_side_effects=True, vmem_limit_bytes=63 * 1024 * 1024
+            collective_id=0, has_side_effects=True, vmem_limit_bytes=56 * 1024 * 1024
         ),
     )(
         stream, skip, norm_gain, norm_shift, conv_weight, mid_gain, mid_shift, mix_weight,

time: 36.4 us -> 31.9 us (0.88)
  Pallas kernels: 34.3 us -> 31.1 us
  local copies, waits for them, and re-layouts: 1.67 us -> 0.71 us
    pallas_call x1, Pallas kernels: 34.3 us -> 31.1 us  [body(): pl.pallas_call(functools.partial(kernel, seq_devices), name='bottleneck',...]
    unnamed x1, local copies, waits for them, and re-layouts: 1.67 us -> 0.71 us
where the time goes in v2:
time: 31.9 us; the launch traced here: 31.8 us
  Pallas kernels  31.1 us (97%)
  local copies, waits for them, and re-layouts  0.71 us (2%)
    pallas_call x1, Pallas kernels, body(): pl.pallas_call(functools.partial(kernel, seq_devices), name='bottleneck',...  31.1 us
    unnamed x1, local copies, waits for them, and re-layouts  0.71 us

profile of v2, /device:TPU:8, one launch (start us, length us, event | category | flops | bytes accessed | tf_op | source)
XLA Modules:
  0.0 31.8 jit_solution(9551919290031571455)
XLA Ops:
  0.0 31.1 %bottleneck.1 = bf16[2,256,256]{2,1,0:T(8,128)(2,1)S(1)} custom-call(bf16[2,64,512]{2,1,0:T(8,128)(2,1)} %stream.1, bf16[2,256,256]{2,1,0:T(8,128)(2,1)} %skip.1, f32[2,1024]{1,0:T(2,128)} %norm_gain.1, f32[2,1024]{1,0:T(2,128)} %norm_shift.1, bf16[2,3,1024,256]{3,2,1,0:T(8,128)(2,1)} %conv_weight.1, f32[2,256]{1,0:T(2,128)} %mid_gain.1, ...), custom_call_target="tpu_custom_call" | custom-call | tf_op jit(solution)/shard_map/bottleneck/pallas_call | solution.py:290
  31.1 0.7 %copy.13 = bf16[2,256,256]{2,1,0:T(8,128)(2,1)} copy(bf16[2,256,256]{2,1,0:T(8,128)(2,1)S(1)} %bottleneck.1) | data formatting | bytes 524288

commit v3 on v2

--- a/solution.py
+++ b/solution.py
@@ -28,8 +28,8 @@
     seq_devices,
     stream, skip, norm_gain, norm_shift, conv_weight, mid_gain, mid_shift, mix_weight, up_gain, up_shift, up_weight,
     out,
-    xr, a0, hb, mw, cw, uw, a1, x1, h1, eh, uf, outf, skipb, ng, ns, mg, ms, ug, us,
-    local_sem, send_sem, recv_sem,
+    xr, a0, hb, mw, cw, uw, a1, x1, h1, eh, uf, outf, zf, cf, accf, skipb, ng, ns, mg, ms, ug, us,
+    local_sem, send_sem, recv_sem, go_sem,
 ):
     s = lax.axis_index("seq")
     g = lax.axis_index("ch")
@@ -38,18 +38,29 @@
     sib_s = s + 1 - 2 * core
     crs_s = lax.rem(s + seq_devices - 1 + 2 * core, seq_devices)
     cut_s = lax.rem(s + seq_devices // 2, seq_devices)
-    x_bit = lax.rem(s // 2, 2)
+    x_at = lax.rem(s // 2, 4)
     z_bit = lax.rem(s // 8, 2)
-    x_step = 2 - 4 * x_bit
+    row = s - 2 * x_at
+    x_next = row + 2 * lax.rem(x_at + 1, 4)
+    x_last = row + 2 * lax.rem(x_at + 3, 4)
     z_step = 8 - 16 * z_bit
+    y_bit = s // (seq_devices // 2)
     has_crs = jnp.logical_and(s > 0, s < seq_devices - 1)
+    ahead = s == seq_devices // 2
+    behind = s == seq_devices // 2 - 1
+    turn = lax.rem(s, 8) == 7 * core
+    at_once = jnp.logical_and(has_crs, jnp.logical_not(ahead))
+    seam = jnp.logical_or(ahead, behind)
+    in_turn = jnp.logical_and(has_crs, jnp.logical_not(seam))
+    direct = jnp.logical_and(has_crs, turn)
+    relayed = jnp.logical_and(has_crs, jnp.logical_not(turn))
     par = {"seq": s, "ch": o}
     sib = {"seq": sib_s, "ch": g}
     crs = {"seq": crs_s, "ch": g}
     dcr = {"seq": crs_s, "ch": o}
     dsb = {"seq": sib_s, "ch": o}
     cut = {"seq": cut_s, "ch": o}
-    mates = [{"seq": s + x_step, "ch": g}, {"seq": s + z_step, "ch": g}, {"seq": s + x_step + z_step, "ch": g}]
+    mates = [{"seq": x_next, "ch": g}, {"seq": x_last, "ch": g}, {"seq": s + z_step, "ch": g}]
     partners = [par, sib, dsb, cut] + mates
 
     barrier = pltpu.get_barrier_semaphore()
@@ -81,7 +92,7 @@
 
     sends = []
 
-    def send(src, dst, device, when=None):
+    def send(src, dst, device, when=None, start=None):
         index = len(sends)
         copy = pltpu.make_async_remote_copy(
             src_ref=src, dst_ref=dst, send_sem=send_sem.at[index], recv_sem=recv_sem.at[index],
@@ -91,18 +102,24 @@
         if when is None:
             copy.start()
         else:
-            pl.when(when)(copy.start)
+            pl.when(when if start is None else start)(copy.start)
         return copy
 
     def arrive(*copies):
         for copy in copies:
             copy.wait_recv()
 
-    def arrive_crs(*copies):
-        @pl.when(has_crs)
+    def arrive_if(when, *copies):
+        @pl.when(when)
         def _():
             for copy in copies:
                 copy.wait_recv()
+
+    def arrive_crs(*copies):
+        arrive_if(has_crs, *copies)
+
+    def weights(n, rows, device):
+        return send(mw.at[n, o, rows], mw.at[n, o, rows], device)
 
     to_sib = 2 * core
     to_crs = 2 - 2 * core
@@ -110,19 +127,37 @@
     my_crs = 2 * core
     near = pl.ds(pl.multiple_of(32 * core, 32), 32)
     far = pl.ds(pl.multiple_of(32 - 32 * core, 32), 32)
-    mine = pl.ds(pl.multiple_of(128 * core, 128), 128)
-    eighth = pl.ds(pl.multiple_of(128 * core + 64 * z_bit + 32 * x_bit, 32), 32)
+
+    def piece(shift):
+        quarter = lax.rem(x_at + 2 * z_bit + shift, 4)
+        return pl.ds(pl.multiple_of(128 * core + 32 * quarter, 32), 32)
+
+    pieces = [piece(0), piece(3), piece(1), piece(2)]
 
     own_copy.wait()
-    pl.semaphore_wait(barrier, jnp.where(has_crs, len(partners) + 2, len(partners)))
-    x_own = xr.at[g, 1]
-    x_par = send(x_own, xr.at[g, 1], par)
-    x_crs = send(xr.at[g, 1, :, near], xr.at[g, to_crs, :, near], crs, has_crs)
-    x_dcr = send(xr.at[g, 1, :, near], xr.at[g, to_crs, :, near], dcr, has_crs)
-    x_sib = send(x_own, xr.at[g, to_sib], sib)
-    w_cut = [send(mix_weight.at[n, eighth], mw.at[n, g, eighth], cut) for n in range(2)]
-    x_crs2 = send(xr.at[g, 1, :, far], xr.at[g, to_crs, :, far], crs, has_crs)
-
+    @pl.when(jnp.logical_not(ahead))
+    def _():
+        pl.semaphore_wait(barrier, jnp.where(has_crs, len(partners) + 2, len(partners)))
+
+    @pl.when(s == 0)
+    def _():
+        pl.semaphore_signal(go_sem, inc=1, device_id=cut, device_id_type=MESH)
+
+    @pl.when(s == seq_devices // 2 + 1)
+    def _():
+        pl.semaphore_signal(go_sem, inc=1, device_id=sib, device_id_type=MESH)
+
+    @pl.when(ahead)
+    def _():
+        pl.semaphore_wait(go_sem, 2)
+
+    x_par = send(xr.at[g, 1, :, near], xr.at[g, 1, :, near], par)
+    x_crs = send(xr.at[g, 1, :, near], xr.at[g, to_crs, :, near], crs, has_crs, at_once)
+    x_dcr = send(xr.at[g, 1, :, near], xr.at[g, to_crs, :, near], dcr, direct, jnp.logical_and(direct, at_once))
+    x_par2 = send(xr.at[g, 1, :, far], xr.at[g, 1, :, far], par)
+    w_cut = [send(mix_weight.at[0, pieces[0]], mw.at[0, g, pieces[0]], cut)]
+    x_sib = send(xr.at[g, 1], xr.at[g, to_sib], sib)
+    x_crs2 = send(xr.at[g, 1, :, far], xr.at[g, to_crs, :, far], crs, has_crs, at_once)
 
     def activate0(gg, slot, rows, dst_row, valid):
         cols = pl.ds(pl.multiple_of(gg * 512, 512), 512)
@@ -156,32 +191,65 @@
     activate0(g, 1, whole, centre, None)
     arrive(x_sib)
     activate0(g, my_sib, sib_src, sib_dst, None)
-    arrive_crs(x_crs)
-    activate0(g, my_crs, crs_src, crs_dst, has_crs)
+    arrive_if(in_turn, x_crs)
+
+    @pl.when(in_turn)
+    def _():
+        activate0(g, my_crs, crs_src, crs_dst, None)
+
+    @pl.when(jnp.logical_not(in_turn))
+    def _():
+        a0[g, :, crs_dst, :] = jnp.zeros((2, 32, 512), BF16)
+
+
+    @pl.when(ahead)
+    def _():
+        pl.semaphore_wait(barrier, len(partners) + 2)
+        x_crs.start()
+        x_dcr.start()
+        x_crs2.start()
+
+    arrive(x_par)
+    x_near = send(xr.at[o, 1, :, near], xr.at[o, to_crs, :, near], crs, relayed)
     cw0_copy.wait()
-    acc = conv0(g)
-    arrive(x_par)
-    x_fwd = send(xr.at[o, 1], xr.at[o, to_sib], sib)
+    accf[...] = conv0(g)
+    arrive(x_par2)
+    x_fwd = send(xr.at[o, 1, :, far], xr.at[o, to_sib, :, far], sib)
+    x_rel = send(xr.at[o, 1, :, far], xr.at[o, to_crs, :, far], crs, has_crs)
     activate0(o, 1, whole, centre, None)
-    arrive_crs(x_dcr)
-    activate0(o, my_crs, crs_src, crs_dst, has_crs)
     arrive(w_cut[0])
-    w_mate = [[send(mw.at[0, o, eighth], mw.at[0, o, eighth], mate) for mate in mates]]
+    w_mate = [[weights(0, pieces[0], mate) for mate in mates]]
+    w_cut.append(send(mix_weight.at[1, pieces[0]], mw.at[1, g, pieces[0]], cut))
+    w_fwd = [[weights(0, pieces[0], sib)]]
+    x_fwd2 = send(xr.at[o, 1, :, near], xr.at[o, to_sib, :, near], sib)
     arrive(x_fwd)
     activate0(o, my_sib, sib_src, sib_dst, None)
-    acc = acc + conv0(o)
+
+    @pl.when(seam)
+    def _():
+        x_crs.wait_recv()
+        activate0(g, my_crs, crs_src, crs_dst, None)
+        accf[...] = conv0(g)
+
+    arrive_if(direct, x_dcr)
+    arrive_if(relayed, x_near)
+    activate0(o, my_crs, crs_src, crs_dst, has_crs)
+    acc = accf[...] + conv0(o)
     hb[g, 1] = gelu(acc * mg[0:1, :] + ms[0:1, :]).astype(BF16)
 
     h_own = hb.at[g, 1]
     h_par = send(h_own, hb.at[g, 1], par)
+    h_dcr = send(h_own, hb.at[g, to_crs], dcr, direct)
     h_crs = send(h_own, hb.at[g, to_crs], crs, has_crs)
-    h_dcr = send(h_own, hb.at[g, to_crs], dcr, has_crs)
     h_sib = send(h_own, hb.at[g, to_sib], sib)
-    x_rel = send(xr.at[o, 1, :, far], xr.at[o, to_crs, :, far], crs, has_crs)
-    arrive(w_cut[1])
-    w_mate.append([send(mw.at[1, o, eighth], mw.at[1, o, eighth], mate) for mate in mates])
-    arrive(*w_mate[0])
-    w_fwd = [send(mw.at[0, o, mine], mw.at[0, o, mine], sib)]
+
+
+    def collect(n):
+        for m in range(3):
+            w_mate[n][m].wait_recv()
+            w_fwd[n].append(weights(n, pieces[m + 1], sib))
+
+    collect(0)
 
     def mix0(slot, valid):
         for n in range(4):
@@ -201,15 +269,21 @@
     cw1_copy.wait()
     arrive(h_par)
     h_fwd = send(hb.at[o, 1], hb.at[o, to_sib], sib)
-    arrive(w_fwd[0])
+    h_rel = send(hb.at[o, 1], hb.at[o, to_crs], crs, relayed)
+    arrive(*w_fwd[0])
     acc = mix0(1, None)
+    arrive(w_cut[1])
+    w_mate.append([weights(1, pieces[0], mate) for mate in mates])
+    w_fwd.append([weights(1, pieces[0], sib)])
     arrive(h_sib)
     arrive(h_fwd)
+    arrive(x_fwd2)
     acc = acc + mix0(my_sib, None)
     arrive_crs(x_crs2)
     arrive_crs(x_rel)
     arrive_crs(h_crs)
-    arrive_crs(h_dcr)
+    arrive_if(direct, h_dcr)
+    arrive_if(relayed, h_rel)
     acc = acc + mix0(my_crs, has_crs)
     h1[g] = gelu(acc * mg[1:2, :] + ms[1:2, :]).astype(BF16).reshape(2, ROWS, 256)
 
@@ -221,61 +295,74 @@
     g_dsb = send(h1.at[g, :, last], eh.at[g, core], dsb)
     g_sib = send(h1.at[g, :, last], eh.at[g, core], sib)
 
-    arrive(*w_mate[1])
-    w_fwd.append(send(mw.at[1, o, mine], mw.at[1, o, mine], sib))
     mw1_copy.wait()
     for copy in up_copies:
         copy.wait()
-    arrive(w_fwd[1])
-
-    def top(h_pair, base, cols):
-        z = dot(h_pair[0], mw[1, 0, :, cols]) + dot(h_pair[1], mw[1, 1, :, cols])
-        x = (base.astype(F32) + z).astype(BF16).astype(F32)
-        v = gelu(x * ug[0:1, cols] + us[0:1, cols])
-        return v.astype(BF16).astype(F32)
-
-    arrive(g_par)
-    for n in range(4):
-        cols = slice(256 * n, 256 * n + 256)
-        u = top([h1[0].reshape(128, 256), h1[1].reshape(128, 256)], x1[1, :, cols], cols)
-        for b in range(2):
-            uf[b, 8 : 8 + ROWS, cols] = u[ROWS * b : ROWS * b + ROWS]
-    arrive(g_sib, g_dsb)
-    arrive_crs(g_crs, g_dcr)
-    for n in range(4):
-        cols = slice(256 * n, 256 * n + 256)
-        for side in range(2):
-            first_row = 48 if side == 0 else 0
-            base = jnp.concatenate(
-                [x1[2 * side, ROWS * b + first_row : ROWS * b + first_row + 16, cols] for b in range(2)], axis=0
-            )
-            u = top([eh[0, side].reshape(32, 256), eh[1, side].reshape(32, 256)], base, cols)
-            u = jnp.where(s > 0 if side == 0 else s < seq_devices - 1, u, 0.0)
+
+    edge_rows = [
+        [slice(ROWS * b + 48 - 48 * side, ROWS * b + 64 - 48 * side) for b in range(2)] for side in range(2)
+    ]
+
+    def half_top(gg, first):
+        for n in range(4):
+            cols = slice(256 * n, 256 * n + 256)
+            z = dot(h1[gg].reshape(128, 256), mw[1, gg, :, cols])
+            if first:
+                zf[:, cols] = z + x1[1, :, cols].astype(F32)
+            else:
+                v = (zf[:, cols] + z).astype(BF16).astype(F32)
+                v = gelu(v * ug[0:1, cols] + us[0:1, cols]).astype(BF16).astype(F32)
+                for b in range(2):
+                    uf[b, 8 : 8 + ROWS, cols] = v[ROWS * b : ROWS * b + ROWS]
+
+    def edge_top():
+        for n in range(4):
+            cols = slice(256 * n, 256 * n + 256)
+            z = dot(eh[0].reshape(64, 256), mw[1, 0, :, cols]) + dot(eh[1].reshape(64, 256), mw[1, 1, :, cols])
+            base = jnp.concatenate([x1[2 * side, rows, cols] for side in range(2) for rows in edge_rows[side]], axis=0)
+            v = (base.astype(F32) + z).astype(BF16).astype(F32)
+            v = gelu(v * ug[0:1, cols] + us[0:1, cols]).astype(BF16).astype(F32)
             for b in range(2):
-                if side == 0:
-                    uf[b, 0:8, cols] = u[16 * b + 8 : 16 * b + 16]
-                else:
-                    uf[b, 8 + ROWS : 16 + ROWS, cols] = u[16 * b : 16 * b + 8]
+                uf[b, 0:8, cols] = jnp.where(s > 0, v[16 * b + 8 : 16 * b + 16], 0.0)
+                uf[b, 8 + ROWS : 16 + ROWS, cols] = jnp.where(
+                    s < seq_devices - 1, v[32 + 16 * b : 32 + 16 * b + 8], 0.0
+                )
 
     def rows_at(offset):
         return jnp.concatenate(
             [uf[b, 8 + offset : 8 + offset + ROWS, :].astype(BF16) for b in range(2)], axis=0
         )
 
-    here, before, after = rows_at(0), rows_at(-1), rows_at(1)
-    for r in range(4):
-        if r < 2:
-            v = dot(here, uw[2 + r]) + dot(before, uw[6 + r])
-        else:
-            v = dot(here, uw[2 + r]) + dot(after, uw[r - 2])
-        for b in range(2):
-            for half in range(2):
-                outf[b, half, pl.ds(r, ROWS, stride=4), :] = v[
-                    ROWS * b : ROWS * b + ROWS, 128 * half : 128 * half + 128
-                ]
-    for half in range(2):
-        lanes = slice(128 * half, 128 * half + 128)
-        out[:, :, lanes] = (outf[:, half] + skipb[:, :, lanes].astype(F32)).astype(BF16)
+    def centre_taps():
+        here = rows_at(0)
+        for r in range(4):
+            cf[r] = dot(here, uw[2 + r])
+
+    def outer_taps():
+        for r in range(4):
+            v = cf[r] + (dot(rows_at(-1), uw[6 + r]) if r < 2 else dot(rows_at(1), uw[r - 2]))
+            for b in range(2):
+                for half in range(2):
+                    outf[b, half, pl.ds(r, ROWS, stride=4), :] = v[
+                        ROWS * b : ROWS * b + ROWS, 128 * half : 128 * half + 128
+                    ]
+
+    def finish():
+        for half in range(2):
+            lanes = slice(128 * half, 128 * half + 128)
+            out[:, :, lanes] = (outf[:, half] + skipb[:, :, lanes].astype(F32)).astype(BF16)
+
+    collect(1)
+    half_top(g, True)
+    arrive(*w_fwd[1])
+    arrive(g_par)
+    half_top(o, False)
+    centre_taps()
+    arrive(g_sib, g_dsb)
+    arrive_crs(g_crs, g_dcr)
+    edge_top()
+    outer_taps()
+    finish()
     for copy, when in sends:
         if when is None:
             copy.wait_send()
@@ -306,6 +393,9 @@
             pltpu.VMEM((2, 2, 2, 16, 256), BF16),
             pltpu.VMEM((2, 80, 1024), F32),
             pltpu.VMEM((2, 2, 256, 128), F32),
+            pltpu.VMEM((128, 1024), F32),
+            pltpu.VMEM((4, 128, 256), F32),
+            pltpu.VMEM((128, 256), F32),
             pltpu.VMEM((2, 256, 256), BF16),
             pltpu.VMEM((2, 1024), F32),
             pltpu.VMEM((2, 1024), F32),
@@ -314,8 +404,9 @@
             pltpu.VMEM((1, 1024), F32),
             pltpu.VMEM((1, 1024), F32),
             pltpu.SemaphoreType.DMA((16,)),
-            pltpu.SemaphoreType.DMA((32,)),
-            pltpu.SemaphoreType.DMA((32,)),
+            pltpu.SemaphoreType.DMA((48,)),
+            pltpu.SemaphoreType.DMA((48,)),
+            pltpu.SemaphoreType.REGULAR,
         ],
         compiler_params=pltpu.CompilerParams(
             collective_id=0, has_side_effects=True, vmem_limit_bytes=56 * 1024 * 1024

time: 31.9 us -> 29.2 us (0.915)
  Pallas kernels: 31.1 us -> 28.4 us
    pallas_call x1, Pallas kernels: 31.1 us -> 28.4 us  [body(): pl.pallas_call(functools.partial(kernel, seq_devices), name='bottleneck',...]
where the time goes in v3:
time: 29.2 us; the launch traced here: 29.1 us
  Pallas kernels  28.4 us (97%)
  local copies, waits for them, and re-layouts  0.71 us (2%)
    pallas_call x1, Pallas kernels, body(): pl.pallas_call(functools.partial(kernel, seq_devices), name='bottleneck',...  28.4 us
    unnamed x1, local copies, waits for them, and re-layouts  0.71 us

profile of v3, /device:TPU:8, one launch (start us, length us, event | category | flops | bytes accessed | tf_op | source)
XLA Modules:
  0.0 29.1 jit_solution(12383552065829558151)
XLA Ops:
  0.0 28.4 %bottleneck.1 = bf16[2,256,256]{2,1,0:T(8,128)(2,1)S(1)} custom-call(bf16[2,64,512]{2,1,0:T(8,128)(2,1)} %stream.1, bf16[2,256,256]{2,1,0:T(8,128)(2,1)} %skip.1, f32[2,1024]{1,0:T(2,128)} %norm_gain.1, f32[2,1024]{1,0:T(2,128)} %norm_shift.1, bf16[2,3,1024,256]{3,2,1,0:T(8,128)(2,1)} %conv_weight.1, f32[2,256]{1,0:T(2,128)} %mid_gain.1, ...), custom_call_target="tpu_custom_call" | custom-call | tf_op jit(solution)/shard_map/bottleneck/pallas_call | solution.py:377
  28.4 0.7 %copy.13 = bf16[2,256,256]{2,1,0:T(8,128)(2,1)} copy(bf16[2,256,256]{2,1,0:T(8,128)(2,1)S(1)} %bottleneck.1) | data formatting | bytes 524288

commit v4 on v3

--- a/solution.py
+++ b/solution.py
@@ -11,6 +11,8 @@
 F32 = jnp.float32
 BF16 = jnp.bfloat16
 ROWS = 64
+LOCALS = 13
+LANDINGS = 21
 GELU_A = 0.7978845608028654
 GELU_B = 0.7978845608028654 * 0.044715
 
@@ -91,11 +93,14 @@
     up_copies = [fetch(up_gain, ug), fetch(up_shift, us), fetch(up_weight, uw), fetch(skip, skipb)]
 
     sends = []
-
-    def send(src, dst, device, when=None, start=None):
-        index = len(sends)
+    names = {}
+
+    def landing(name):
+        return recv_sem.at[names.setdefault(name, len(names))]
+
+    def send(name, src, dst, device, when=None, start=None):
         copy = pltpu.make_async_remote_copy(
-            src_ref=src, dst_ref=dst, send_sem=send_sem.at[index], recv_sem=recv_sem.at[index],
+            src_ref=src, dst_ref=dst, send_sem=send_sem.at[0], recv_sem=landing(name),
             device_id=device, device_id_type=MESH,
         )
         sends.append((copy, when))
@@ -105,21 +110,29 @@
             pl.when(when if start is None else start)(copy.start)
         return copy
 
-    def arrive(*copies):
-        for copy in copies:
-            copy.wait_recv()
-
-    def arrive_if(when, *copies):
-        @pl.when(when)
-        def _():
-            for copy in copies:
-                copy.wait_recv()
-
-    def arrive_crs(*copies):
-        arrive_if(has_crs, *copies)
-
-    def weights(n, rows, device):
-        return send(mw.at[n, o, rows], mw.at[n, o, rows], device)
+    def arrive(name, block):
+        pltpu.make_async_remote_copy(
+            src_ref=block, dst_ref=block, send_sem=send_sem.at[0], recv_sem=landing(name),
+            device_id=par, device_id_type=MESH,
+        ).wait_recv()
+
+    def arrive_if(when, name, block):
+        pl.when(when)(functools.partial(arrive, name, block))
+
+    def weights(name, n, rows, device):
+        return send(name, mw.at[n, o, rows], mw.at[n, o, rows], device)
+
+    def drain():
+        for copy, when in sends:
+            if when is None:
+                copy.wait_send()
+        for group in (has_crs, direct, relayed):
+            some = [copy for copy, when in sends if when is group]
+
+            @pl.when(group)
+            def _():
+                for copy in some:
+                    copy.wait_send()
 
     to_sib = 2 * core
     to_crs = 2 - 2 * core
@@ -132,6 +145,8 @@
         quarter = lax.rem(x_at + 2 * z_bit + shift, 4)
         return pl.ds(pl.multiple_of(128 * core + 32 * quarter, 32), 32)
 
+    mine = pl.ds(pl.multiple_of(128 * core, 128), 128)
+    theirs = pl.ds(pl.multiple_of(128 - 128 * core, 128), 128)
     pieces = [piece(0), piece(3), piece(1), piece(2)]
 
     own_copy.wait()
@@ -151,13 +166,14 @@
     def _():
         pl.semaphore_wait(go_sem, 2)
 
-    x_par = send(xr.at[g, 1, :, near], xr.at[g, 1, :, near], par)
-    x_crs = send(xr.at[g, 1, :, near], xr.at[g, to_crs, :, near], crs, has_crs, at_once)
-    x_dcr = send(xr.at[g, 1, :, near], xr.at[g, to_crs, :, near], dcr, direct, jnp.logical_and(direct, at_once))
-    x_par2 = send(xr.at[g, 1, :, far], xr.at[g, 1, :, far], par)
-    w_cut = [send(mix_weight.at[0, pieces[0]], mw.at[0, g, pieces[0]], cut)]
-    x_sib = send(xr.at[g, 1], xr.at[g, to_sib], sib)
-    x_crs2 = send(xr.at[g, 1, :, far], xr.at[g, to_crs, :, far], crs, has_crs, at_once)
+    for b in range(2):
+        send(f"x_par{b}", xr.at[g, 1, b, near], xr.at[g, 1, b, near], par)
+    x_crs = send("x_crs", xr.at[g, 1, :, near], xr.at[g, to_crs, :, near], crs, has_crs, at_once)
+    x_dcr = send("x_near", xr.at[g, 1, :, near], xr.at[g, to_crs, :, near], dcr, direct, jnp.logical_and(direct, at_once))
+    send("x_par2", xr.at[g, 1, :, far], xr.at[g, 1, :, far], par)
+    send("w_cut0", mix_weight.at[0, pieces[0]], mw.at[0, g, pieces[0]], cut)
+    send("x_sib", xr.at[g, 1], xr.at[g, to_sib], sib)
+    x_crs2 = send("x_far", xr.at[g, 1, :, far], xr.at[g, to_crs, :, far], crs, has_crs, at_once)
 
     def activate0(gg, slot, rows, dst_row, valid):
         cols = pl.ds(pl.multiple_of(gg * 512, 512), 512)
@@ -189,9 +205,9 @@
     for copy in gain_copies:
         copy.wait()
     activate0(g, 1, whole, centre, None)
-    arrive(x_sib)
+    arrive("x_sib", xr.at[g, my_sib])
     activate0(g, my_sib, sib_src, sib_dst, None)
-    arrive_if(in_turn, x_crs)
+    arrive_if(in_turn, "x_crs", xr.at[g, my_crs, :, far])
 
     @pl.when(in_turn)
     def _():
@@ -200,7 +216,6 @@
     @pl.when(jnp.logical_not(in_turn))
     def _():
         a0[g, :, crs_dst, :] = jnp.zeros((2, 32, 512), BF16)
-
 
     @pl.when(ahead)
     def _():
@@ -209,47 +224,44 @@
         x_dcr.start()
         x_crs2.start()
 
-    arrive(x_par)
-    x_near = send(xr.at[o, 1, :, near], xr.at[o, to_crs, :, near], crs, relayed)
+    for b in range(2):
+        arrive(f"x_par{b}", xr.at[o, 1, b, near])
+        send("x_near", xr.at[o, 1, b, near], xr.at[o, to_crs, b, near], crs, relayed)
     cw0_copy.wait()
     accf[...] = conv0(g)
-    arrive(x_par2)
-    x_fwd = send(xr.at[o, 1, :, far], xr.at[o, to_sib, :, far], sib)
-    x_rel = send(xr.at[o, 1, :, far], xr.at[o, to_crs, :, far], crs, has_crs)
+    arrive("x_par2", xr.at[o, 1, :, far])
+    send("x_fwd", xr.at[o, 1, :, far], xr.at[o, to_sib, :, far], sib)
+    send("x_far", xr.at[o, 1, :, far], xr.at[o, to_crs, :, far], crs, has_crs)
     activate0(o, 1, whole, centre, None)
-    arrive(w_cut[0])
-    w_mate = [[weights(0, pieces[0], mate) for mate in mates]]
-    w_cut.append(send(mix_weight.at[1, pieces[0]], mw.at[1, g, pieces[0]], cut))
-    w_fwd = [[weights(0, pieces[0], sib)]]
-    x_fwd2 = send(xr.at[o, 1, :, near], xr.at[o, to_sib, :, near], sib)
-    arrive(x_fwd)
+    arrive("w_cut0", mw.at[0, o, pieces[0]])
+    for m in range(3):
+        weights(f"w_mate{m}", 0, pieces[0], mates[m])
+    send("w_cut1", mix_weight.at[1, pieces[0]], mw.at[1, g, pieces[0]], cut)
+    weights("w_fwd0", 0, pieces[0], sib)
+    send("x_fwd2", xr.at[o, 1, :, near], xr.at[o, to_sib, :, near], sib)
+    arrive("x_fwd", xr.at[o, my_sib, :, near])
     activate0(o, my_sib, sib_src, sib_dst, None)
 
     @pl.when(seam)
     def _():
-        x_crs.wait_recv()
+        arrive("x_crs", xr.at[g, my_crs, :, far])
         activate0(g, my_crs, crs_src, crs_dst, None)
         accf[...] = conv0(g)
 
-    arrive_if(direct, x_dcr)
-    arrive_if(relayed, x_near)
+    arrive_if(has_crs, "x_near", xr.at[o, my_crs, :, far])
     activate0(o, my_crs, crs_src, crs_dst, has_crs)
     acc = accf[...] + conv0(o)
     hb[g, 1] = gelu(acc * mg[0:1, :] + ms[0:1, :]).astype(BF16)
 
-    h_own = hb.at[g, 1]
-    h_par = send(h_own, hb.at[g, 1], par)
-    h_dcr = send(h_own, hb.at[g, to_crs], dcr, direct)
-    h_crs = send(h_own, hb.at[g, to_crs], crs, has_crs)
-    h_sib = send(h_own, hb.at[g, to_sib], sib)
-
-
-    def collect(n):
-        for m in range(3):
-            w_mate[n][m].wait_recv()
-            w_fwd[n].append(weights(n, pieces[m + 1], sib))
-
-    collect(0)
+    halves = [pl.ds(ROWS * b, ROWS) for b in range(2)]
+    for b in range(2):
+        send(f"h_par{b}", hb.at[g, 1, halves[b]], hb.at[g, 1, halves[b]], par)
+    send("h_crs", hb.at[g, 1], hb.at[g, to_crs], dcr, direct)
+    send("h_crs", hb.at[g, 1], hb.at[g, to_crs], crs, has_crs)
+    send("h_sib", hb.at[g, 1], hb.at[g, to_sib], sib)
+    for m in range(3):
+        arrive(f"w_mate{m}", mw.at[0, o, pieces[m + 1]])
+        weights("w_fwd0", 0, pieces[m + 1], sib)
 
     def mix0(slot, valid):
         for n in range(4):
@@ -267,33 +279,30 @@
 
     mw0_copy.wait()
     cw1_copy.wait()
-    arrive(h_par)
-    h_fwd = send(hb.at[o, 1], hb.at[o, to_sib], sib)
-    h_rel = send(hb.at[o, 1], hb.at[o, to_crs], crs, relayed)
-    arrive(*w_fwd[0])
+    for b in range(2):
+        arrive(f"h_par{b}", hb.at[o, 1, halves[b]])
+        send("h_crs", hb.at[o, 1, halves[b]], hb.at[o, to_crs, halves[b]], crs, relayed)
+        send("h_sib", hb.at[o, 1, halves[b]], hb.at[o, to_sib, halves[b]], sib)
+    arrive("w_fwd0", mw.at[0, o, theirs])
     acc = mix0(1, None)
-    arrive(w_cut[1])
-    w_mate.append([weights(1, pieces[0], mate) for mate in mates])
-    w_fwd.append([weights(1, pieces[0], sib)])
-    arrive(h_sib)
-    arrive(h_fwd)
-    arrive(x_fwd2)
+    arrive("w_cut1", mw.at[1, o, pieces[0]])
+    for mate in mates:
+        weights("w_mate", 1, pieces[0], mate)
+    arrive("h_sib", hb.at[:, my_sib])
+    arrive("x_fwd2", xr.at[o, my_sib, :, far])
     acc = acc + mix0(my_sib, None)
-    arrive_crs(x_crs2)
-    arrive_crs(x_rel)
-    arrive_crs(h_crs)
-    arrive_if(direct, h_dcr)
-    arrive_if(relayed, h_rel)
+    arrive_if(has_crs, "x_far", xr.at[:, my_crs, :, near])
+    arrive_if(has_crs, "h_crs", hb.at[:, my_crs])
     acc = acc + mix0(my_crs, has_crs)
     h1[g] = gelu(acc * mg[1:2, :] + ms[1:2, :]).astype(BF16).reshape(2, ROWS, 256)
 
     last = pl.ds(pl.multiple_of(48 - 48 * core, 16), 16)
     first = pl.ds(pl.multiple_of(48 * core, 16), 16)
-    g_par = send(h1.at[g], h1.at[g], par)
-    g_crs = send(h1.at[g, :, first], eh.at[g, 1 - core], crs, has_crs)
-    g_dcr = send(h1.at[g, :, first], eh.at[g, 1 - core], dcr, has_crs)
-    g_dsb = send(h1.at[g, :, last], eh.at[g, core], dsb)
-    g_sib = send(h1.at[g, :, last], eh.at[g, core], sib)
+    send("x_par0", h1.at[g], h1.at[g], par)
+    send("x_crs", h1.at[g, :, first], eh.at[g, 1 - core], crs, has_crs)
+    send("x_crs", h1.at[g, :, first], eh.at[g, 1 - core], dcr, has_crs)
+    send("x_sib", h1.at[g, :, last], eh.at[g, core], dsb)
+    send("x_sib", h1.at[g, :, last], eh.at[g, core], sib)
 
     mw1_copy.wait()
     for copy in up_copies:
@@ -352,22 +361,20 @@
             lanes = slice(128 * half, 128 * half + 128)
             out[:, :, lanes] = (outf[:, half] + skipb[:, :, lanes].astype(F32)).astype(BF16)
 
-    collect(1)
+    arrive("w_mate", mw.at[1, o, pl.ds(0, 96)])
+    weights("w_fwd1", 1, mine, sib)
     half_top(g, True)
-    arrive(*w_fwd[1])
-    arrive(g_par)
+    arrive("w_fwd1", mw.at[1, o, theirs])
+    arrive("x_par0", h1.at[o])
     half_top(o, False)
     centre_taps()
-    arrive(g_sib, g_dsb)
-    arrive_crs(g_crs, g_dcr)
+    arrive("x_sib", eh.at[:, 1 - core])
+    arrive_if(has_crs, "x_crs", eh.at[:, core])
     edge_top()
     outer_taps()
     finish()
-    for copy, when in sends:
-        if when is None:
-            copy.wait_send()
-        else:
-            pl.when(when)(copy.wait_send)
+    drain()
+    assert len(names) == LANDINGS and len(local) == LOCALS
 
 
 def body(
@@ -403,9 +410,9 @@
             pltpu.VMEM((2, 256), F32),
             pltpu.VMEM((1, 1024), F32),
             pltpu.VMEM((1, 1024), F32),
-            pltpu.SemaphoreType.DMA((16,)),
-            pltpu.SemaphoreType.DMA((48,)),
-            pltpu.SemaphoreType.DMA((48,)),
+            pltpu.SemaphoreType.DMA((LOCALS,)),
+            pltpu.SemaphoreType.DMA((1,)),
+            pltpu.SemaphoreType.DMA((LANDINGS,)),
             pltpu.SemaphoreType.REGULAR,
         ],
         compiler_params=pltpu.CompilerParams(

time: 29.2 us -> 28.4 us (0.973)
  Pallas kernels: 28.4 us -> 27.6 us
    pallas_call x1, Pallas kernels: 28.4 us -> 27.6 us  [body(): pl.pallas_call(functools.partial(kernel, seq_devices), name='bottleneck',...]
where the time goes in v4:
time: 28.4 us; the launch traced here: 28.3 us
  Pallas kernels  27.6 us (97%)
  local copies, waits for them, and re-layouts  0.71 us (2%)
    pallas_call x1, Pallas kernels, body(): pl.pallas_call(functools.partial(kernel, seq_devices), name='bottleneck',...  27.6 us
    unnamed x1, local copies, waits for them, and re-layouts  0.71 us

profile of v4, /device:TPU:8, one launch (start us, length us, event | category | flops | bytes accessed | tf_op | source)
XLA Modules:
  0.0 28.3 jit_solution(2918682469123396001)
XLA Ops:
  0.0 27.6 %bottleneck.1 = bf16[2,256,256]{2,1,0:T(8,128)(2,1)S(1)} custom-call(bf16[2,64,512]{2,1,0:T(8,128)(2,1)} %stream.1, bf16[2,256,256]{2,1,0:T(8,128)(2,1)} %skip.1, f32[2,1024]{1,0:T(2,128)} %norm_gain.1, f32[2,1024]{1,0:T(2,128)} %norm_shift.1, bf16[2,3,1024,256]{3,2,1,0:T(8,128)(2,1)} %conv_weight.1, f32[2,256]{1,0:T(2,128)} %mid_gain.1, ...), custom_call_target="tpu_custom_call" | custom-call | tf_op jit(solution)/shard_map/bottleneck/pallas_call | solution.py:384
  27.6 0.7 %copy.13 = bf16[2,256,256]{2,1,0:T(8,128)(2,1)} copy(bf16[2,256,256]{2,1,0:T(8,128)(2,1)S(1)} %bottleneck.1) | data formatting | bytes 524288

commit v5 on v4

--- a/solution.py
+++ b/solution.py
@@ -12,7 +12,7 @@
 BF16 = jnp.bfloat16
 ROWS = 64
 LOCALS = 13
-LANDINGS = 21
+LANDINGS = 26
 GELU_A = 0.7978845608028654
 GELU_B = 0.7978845608028654 * 0.044715
 
@@ -30,8 +30,8 @@
     seq_devices,
     stream, skip, norm_gain, norm_shift, conv_weight, mid_gain, mid_shift, mix_weight, up_gain, up_shift, up_weight,
     out,
-    xr, a0, hb, mw, cw, uw, a1, x1, h1, eh, uf, outf, zf, cf, accf, skipb, ng, ns, mg, ms, ug, us,
-    local_sem, send_sem, recv_sem, go_sem,
+    xr, a0, hb, mw, cw, uw, a1, x1, h1, eh, ex, eg, ea, uf, outf, zf, cf, accf, skipb, ng, ns, mg, ms, ug, us,
+    local_sem, send_sem, recv_sem, go_sem, known_sem,
 ):
     s = lax.axis_index("seq")
     g = lax.axis_index("ch")
@@ -53,8 +53,11 @@
     turn = lax.rem(s, 8) == 7 * core
     at_once = jnp.logical_and(has_crs, jnp.logical_not(ahead))
     seam = jnp.logical_or(ahead, behind)
+    feeder = s == seq_devices // 2 - 2
+    crs_edges = jnp.logical_and(has_crs, jnp.logical_not(behind))
     in_turn = jnp.logical_and(has_crs, jnp.logical_not(seam))
     direct = jnp.logical_and(has_crs, turn)
+    direct_edges = jnp.logical_and(direct, jnp.logical_not(behind))
     relayed = jnp.logical_and(has_crs, jnp.logical_not(turn))
     par = {"seq": s, "ch": o}
     sib = {"seq": sib_s, "ch": g}
@@ -63,16 +66,19 @@
     dsb = {"seq": sib_s, "ch": o}
     cut = {"seq": cut_s, "ch": o}
     mates = [{"seq": x_next, "ch": g}, {"seq": x_last, "ch": g}, {"seq": s + z_step, "ch": g}]
-    partners = [par, sib, dsb, cut] + mates
+    partners = [par, sib, cut] + mates
+    middle = s // 2 == seq_devices // 4
 
     barrier = pltpu.get_barrier_semaphore()
     for device in partners:
         pl.semaphore_signal(barrier, inc=1, device_id=device, device_id_type=MESH)
 
-    @pl.when(has_crs)
-    def _():
-        for device in (crs, dcr):
-            pl.semaphore_signal(barrier, inc=1, device_id=device, device_id_type=MESH)
+    back = [{"seq": lax.rem(s + seq_devices - 2, seq_devices), "ch": ch} for ch in (g, o)]
+    fed = [{"seq": lax.rem(s + 2, seq_devices), "ch": ch} for ch in (g, o)]
+    for device, when in ((crs, has_crs), (dcr, direct), (dsb, middle), (back[0], ahead), (back[1], ahead)):
+        pl.when(when)(functools.partial(
+            pl.semaphore_signal, barrier, inc=1, device_id=device, device_id_type=MESH
+        ))
 
     local = []
 
@@ -126,7 +132,7 @@
         for copy, when in sends:
             if when is None:
                 copy.wait_send()
-        for group in (has_crs, direct, relayed):
+        for group in (has_crs, direct, relayed, ahead, crs_edges, direct_edges, feeder):
             some = [copy for copy, when in sends if when is group]
 
             @pl.when(group)
@@ -145,14 +151,16 @@
         quarter = lax.rem(x_at + 2 * z_bit + shift, 4)
         return pl.ds(pl.multiple_of(128 * core + 32 * quarter, 32), 32)
 
-    mine = pl.ds(pl.multiple_of(128 * core, 128), 128)
     theirs = pl.ds(pl.multiple_of(128 - 128 * core, 128), 128)
     pieces = [piece(0), piece(3), piece(1), piece(2)]
 
     own_copy.wait()
+    entered = len(partners) + has_crs.astype(jnp.int32) + direct.astype(jnp.int32) + middle.astype(jnp.int32)
+    entered = entered + 2 * feeder.astype(jnp.int32)
+
     @pl.when(jnp.logical_not(ahead))
     def _():
-        pl.semaphore_wait(barrier, jnp.where(has_crs, len(partners) + 2, len(partners)))
+        pl.semaphore_wait(barrier, entered)
 
     @pl.when(s == 0)
     def _():
@@ -165,6 +173,14 @@
     @pl.when(ahead)
     def _():
         pl.semaphore_wait(go_sem, 2)
+
+    def vouch():
+        pl.semaphore_signal(known_sem, inc=1, device_id=sib, device_id_type=MESH)
+        pl.when(has_crs)(functools.partial(
+            pl.semaphore_signal, known_sem, inc=1, device_id=crs, device_id_type=MESH
+        ))
+
+    pl.when(jnp.logical_not(ahead))(vouch)
 
     for b in range(2):
         send(f"x_par{b}", xr.at[g, 1, b, near], xr.at[g, 1, b, near], par)
@@ -174,6 +190,8 @@
     send("w_cut0", mix_weight.at[0, pieces[0]], mw.at[0, g, pieces[0]], cut)
     send("x_sib", xr.at[g, 1], xr.at[g, to_sib], sib)
     x_crs2 = send("x_far", xr.at[g, 1, :, far], xr.at[g, to_crs, :, far], crs, has_crs, at_once)
+    for device in fed:
+        send("x_feed", xr.at[g, 1, :, pl.ds(48, 16)], ex.at[g], device, feeder)
 
     def activate0(gg, slot, rows, dst_row, valid):
         cols = pl.ds(pl.multiple_of(gg * 512, 512), 512)
@@ -219,10 +237,9 @@
 
     @pl.when(ahead)
     def _():
-        pl.semaphore_wait(barrier, len(partners) + 2)
+        pl.semaphore_wait(barrier, entered)
         x_crs.start()
         x_dcr.start()
-        x_crs2.start()
 
     for b in range(2):
         arrive(f"x_par{b}", xr.at[o, 1, b, near])
@@ -232,16 +249,19 @@
     arrive("x_par2", xr.at[o, 1, :, far])
     send("x_fwd", xr.at[o, 1, :, far], xr.at[o, to_sib, :, far], sib)
     send("x_far", xr.at[o, 1, :, far], xr.at[o, to_crs, :, far], crs, has_crs)
+    send("w_cut1", mix_weight.at[1, pieces[0]], mw.at[1, g, pieces[0]], cut)
     activate0(o, 1, whole, centre, None)
     arrive("w_cut0", mw.at[0, o, pieces[0]])
     for m in range(3):
         weights(f"w_mate{m}", 0, pieces[0], mates[m])
-    send("w_cut1", mix_weight.at[1, pieces[0]], mw.at[1, g, pieces[0]], cut)
     weights("w_fwd0", 0, pieces[0], sib)
     send("x_fwd2", xr.at[o, 1, :, near], xr.at[o, to_sib, :, near], sib)
     arrive("x_fwd", xr.at[o, my_sib, :, near])
     activate0(o, my_sib, sib_src, sib_dst, None)
 
+    pl.when(ahead)(x_crs2.start)
+    pl.when(ahead)(vouch)
+
     @pl.when(seam)
     def _():
         arrive("x_crs", xr.at[g, my_crs, :, far])
@@ -255,54 +275,86 @@
 
     halves = [pl.ds(ROWS * b, ROWS) for b in range(2)]
     for b in range(2):
+        send(f"h_crs{b}", hb.at[g, 1, halves[b]], hb.at[g, to_crs, halves[b]], dcr, direct)
+    for b in range(2):
         send(f"h_par{b}", hb.at[g, 1, halves[b]], hb.at[g, 1, halves[b]], par)
-    send("h_crs", hb.at[g, 1], hb.at[g, to_crs], dcr, direct)
-    send("h_crs", hb.at[g, 1], hb.at[g, to_crs], crs, has_crs)
+    for b in range(2):
+        send(f"h_crs{b}", hb.at[g, 1, halves[b]], hb.at[g, to_crs, halves[b]], crs, has_crs)
     send("h_sib", hb.at[g, 1], hb.at[g, to_sib], sib)
+    for device in fed:
+        for b in range(2):
+            send("h_feed", hb.at[g, 1, pl.ds(ROWS * b + 48, 16)], eg.at[g, pl.ds(16 * b, 16)], device, feeder)
     for m in range(3):
         arrive(f"w_mate{m}", mw.at[0, o, pieces[m + 1]])
         weights("w_fwd0", 0, pieces[m + 1], sib)
 
-    def mix0(slot, valid):
+    def mix0(slot, valid, rows, batch):
+        count = rows.stop - rows.start
         for n in range(4):
             cols = slice(256 * n, 256 * n + 256)
             gg, inner = n // 2, slice(256 * (n % 2), 256 * (n % 2) + 256)
-            z = dot(hb[0, slot], mw[0, 0, :, cols]) + dot(hb[1, slot], mw[0, 1, :, cols])
-            x = xr[gg, slot, :, :, inner].reshape(128, 256).astype(F32) + z
+            z = dot(hb[0, slot, rows], mw[0, 0, :, cols]) + dot(hb[1, slot, rows], mw[0, 1, :, cols])
+            x = xr[gg, slot, batch, :, inner].reshape(count, 256).astype(F32) + z
             x = x.astype(BF16)
-            x1[slot, :, cols] = x
+            x1[slot, rows, cols] = x
             v = gelu(x.astype(F32) * ng[1:2, cols] + ns[1:2, cols])
             if valid is not None:
                 v = jnp.where(valid, v, 0.0)
-            a1[slot, :, cols] = v.astype(BF16)
-        return dot(a1[slot], cw[1, slot])
-
+            a1[slot, rows, cols] = v.astype(BF16)
+        return dot(a1[slot, rows], cw[1, slot])
+
+    last = pl.ds(pl.multiple_of(48 - 48 * core, 16), 16)
+    first = pl.ds(pl.multiple_of(48 * core, 16), 16)
+    every = slice(0, 128)
+    both = slice(0, 2)
     mw0_copy.wait()
     cw1_copy.wait()
     for b in range(2):
         arrive(f"h_par{b}", hb.at[o, 1, halves[b]])
-        send("h_crs", hb.at[o, 1, halves[b]], hb.at[o, to_crs, halves[b]], crs, relayed)
+        send(f"h_crs{b}", hb.at[o, 1, halves[b]], hb.at[o, to_crs, halves[b]], crs, relayed)
         send("h_sib", hb.at[o, 1, halves[b]], hb.at[o, to_sib, halves[b]], sib)
+    arrive("w_cut1", mw.at[1, o, pieces[0]])
+    for m in range(3):
+        weights(f"w_mate{m + 3}", 1, pieces[0], mates[m])
+    weights("w_fwd1", 1, pieces[0], sib)
     arrive("w_fwd0", mw.at[0, o, theirs])
-    acc = mix0(1, None)
-    arrive("w_cut1", mw.at[1, o, pieces[0]])
-    for mate in mates:
-        weights("w_mate", 1, pieces[0], mate)
+    acc = mix0(1, None, every, both)
     arrive("h_sib", hb.at[:, my_sib])
     arrive("x_fwd2", xr.at[o, my_sib, :, far])
-    acc = acc + mix0(my_sib, None)
+    acc = acc + mix0(my_sib, None, every, both)
     arrive_if(has_crs, "x_far", xr.at[:, my_crs, :, near])
-    arrive_if(has_crs, "h_crs", hb.at[:, my_crs])
-    acc = acc + mix0(my_crs, has_crs)
-    h1[g] = gelu(acc * mg[1:2, :] + ms[1:2, :]).astype(BF16).reshape(2, ROWS, 256)
-
-    last = pl.ds(pl.multiple_of(48 - 48 * core, 16), 16)
-    first = pl.ds(pl.multiple_of(48 * core, 16), 16)
-    send("x_par0", h1.at[g], h1.at[g], par)
-    send("x_crs", h1.at[g, :, first], eh.at[g, 1 - core], crs, has_crs)
-    send("x_crs", h1.at[g, :, first], eh.at[g, 1 - core], dcr, has_crs)
+    for b in range(2):
+        rows = slice(ROWS * b, ROWS * b + ROWS)
+        arrive_if(has_crs, f"h_crs{b}", hb.at[:, my_crs, rows])
+        part = acc[rows] + mix0(my_crs, has_crs, rows, slice(b, b + 1))
+        h1[g, b] = gelu(part * mg[1:2, :] + ms[1:2, :]).astype(BF16)
+        if b == 1:
+            send("x_crs", h1.at[g, :, first], eh.at[g, 1 - core], dcr, direct_edges)
+        send(f"x_par{b}", h1.at[g, b], h1.at[g, b], par)
+
+    pl.semaphore_wait(known_sem, 1 + has_crs.astype(jnp.int32))
+    send("x_crs", h1.at[g, :, first], eh.at[g, 1 - core], crs, crs_edges)
+    send("x_crs", h1.at[g, :, first], eh.at[g, 1 - core], dcr, relayed)
     send("x_sib", h1.at[g, :, last], eh.at[g, core], dsb)
     send("x_sib", h1.at[g, :, last], eh.at[g, core], sib)
+
+    def edge_behind():
+        arrive("x_feed", ex)
+        arrive("h_feed", eg)
+        for n in range(4):
+            cols = slice(256 * n, 256 * n + 256)
+            gg, inner = n // 2, slice(256 * (n % 2), 256 * (n % 2) + 256)
+            z = dot(eg[0], mw[0, 0, :, cols]) + dot(eg[1], mw[0, 1, :, cols])
+            x = (ex[gg, :, :, inner].reshape(32, 256).astype(F32) + z).astype(BF16).astype(F32)
+            ea[:, cols] = gelu(x * ng[1:2, cols] + ns[1:2, cols]).astype(BF16)
+        y = dot(ea[...], cw[1, 0])
+        for k in range(2):
+            tail = jnp.concatenate([a1[k, ROWS * b + 48 : ROWS * b + ROWS, :] for b in range(2)], axis=0)
+            y = y + dot(tail, cw[1, k + 1])
+        eh[g, 0] = gelu(y * mg[1:2, :] + ms[1:2, :]).astype(BF16).reshape(2, 16, 256)
+
+    pl.when(ahead)(edge_behind)
+    send("x_crs", eh.at[g, 0], eh.at[g, 0], par, ahead)
 
     mw1_copy.wait()
     for copy in up_copies:
@@ -312,17 +364,18 @@
         [slice(ROWS * b + 48 - 48 * side, ROWS * b + 64 - 48 * side) for b in range(2)] for side in range(2)
     ]
 
-    def half_top(gg, first):
+    def half_top():
         for n in range(4):
             cols = slice(256 * n, 256 * n + 256)
-            z = dot(h1[gg].reshape(128, 256), mw[1, gg, :, cols])
-            if first:
-                zf[:, cols] = z + x1[1, :, cols].astype(F32)
-            else:
-                v = (zf[:, cols] + z).astype(BF16).astype(F32)
-                v = gelu(v * ug[0:1, cols] + us[0:1, cols]).astype(BF16).astype(F32)
-                for b in range(2):
-                    uf[b, 8 : 8 + ROWS, cols] = v[ROWS * b : ROWS * b + ROWS]
+            zf[:, cols] = dot(h1[g].reshape(128, 256), mw[1, g, :, cols]) + x1[1, :, cols].astype(F32)
+
+    def whole_top(b):
+        rows = slice(ROWS * b, ROWS * b + ROWS)
+        for n in range(4):
+            cols = slice(256 * n, 256 * n + 256)
+            v = (zf[rows, cols] + dot(h1[o, b], mw[1, o, :, cols])).astype(BF16).astype(F32)
+            v = gelu(v * ug[0:1, cols] + us[0:1, cols])
+            uf[b, 8 : 8 + ROWS, cols] = v.astype(BF16).astype(F32)
 
     def edge_top():
         for n in range(4):
@@ -361,15 +414,18 @@
             lanes = slice(128 * half, 128 * half + 128)
             out[:, :, lanes] = (outf[:, half] + skipb[:, :, lanes].astype(F32)).astype(BF16)
 
-    arrive("w_mate", mw.at[1, o, pl.ds(0, 96)])
-    weights("w_fwd1", 1, mine, sib)
-    half_top(g, True)
+    for m in range(3):
+        arrive(f"w_mate{m + 3}", mw.at[1, o, pieces[m + 1]])
+        weights("w_fwd1", 1, pieces[m + 1], sib)
+    half_top()
     arrive("w_fwd1", mw.at[1, o, theirs])
-    arrive("x_par0", h1.at[o])
-    half_top(o, False)
+    for b in range(2):
+        arrive(f"x_par{b}", h1.at[o, b])
+        whole_top(b)
     centre_taps()
     arrive("x_sib", eh.at[:, 1 - core])
-    arrive_if(has_crs, "x_crs", eh.at[:, core])
+    arrive_if(at_once, "x_crs", eh.at[:, core])
+    arrive_if(ahead, "x_crs", eh.at[o, core])
     edge_top()
     outer_taps()
     finish()
@@ -398,6 +454,9 @@
             pltpu.VMEM((3, 128, 1024), BF16),
             pltpu.VMEM((2, 2, 64, 256), BF16),
             pltpu.VMEM((2, 2, 2, 16, 256), BF16),
+            pltpu.VMEM((2, 2, 16, 512), BF16),
+            pltpu.VMEM((2, 32, 256), BF16),
+            pltpu.VMEM((32, 1024), BF16),
             pltpu.VMEM((2, 80, 1024), F32),
             pltpu.VMEM((2, 2, 256, 128), F32),
             pltpu.VMEM((128, 1024), F32),
@@ -413,6 +472,7 @@
             pltpu.SemaphoreType.DMA((LOCALS,)),
             pltpu.SemaphoreType.DMA((1,)),
             pltpu.SemaphoreType.DMA((LANDINGS,)),
+            pltpu.SemaphoreType.REGULAR,
             pltpu.SemaphoreType.REGULAR,
         ],
         compiler_params=pltpu.CompilerParams(

time: 28.4 us -> 27.9 us (0.982); the launches traced: 28.3 us -> 27.5 us
  Pallas kernels: 27.6 us -> 26.8 us
    pallas_call x1, Pallas kernels: 27.6 us -> 26.8 us  [body(): pl.pallas_call(functools.partial(kernel, seq_devices), name='bottleneck',...]
where the time goes in v5:
time: 27.9 us; the launch traced here: 27.5 us
  Pallas kernels  26.8 us (96%)
  local copies, waits for them, and re-layouts  0.71 us (3%)
    pallas_call x1, Pallas kernels, body(): pl.pallas_call(functools.partial(kernel, seq_devices), name='bottleneck',...  26.8 us
    unnamed x1, local copies, waits for them, and re-layouts  0.71 us

profile of v5, /device:TPU:8, one launch (start us, length us, event | category | flops | bytes accessed | tf_op | source)
XLA Modules:
  0.0 27.5 jit_solution(18242581627808106381)
XLA Ops:
  0.0 26.8 %bottleneck.1 = bf16[2,256,256]{2,1,0:T(8,128)(2,1)S(1)} custom-call(bf16[2,64,512]{2,1,0:T(8,128)(2,1)} %stream.1, bf16[2,256,256]{2,1,0:T(8,128)(2,1)} %skip.1, f32[2,1024]{1,0:T(2,128)} %norm_gain.1, f32[2,1024]{1,0:T(2,128)} %norm_shift.1, bf16[2,3,1024,256]{3,2,1,0:T(8,128)(2,1)} %conv_weight.1, f32[2,256]{1,0:T(2,128)} %mid_gain.1, ...), custom_call_target="tpu_custom_call" | custom-call | tf_op jit(solution)/shard_map/bottleneck/pallas_call | solution.py:440
  26.8 0.7 %copy.13 = bf16[2,256,256]{2,1,0:T(8,128)(2,1)} copy(bf16[2,256,256]{2,1,0:T(8,128)(2,1)S(1)} %bottleneck.1) | data formatting | bytes 524288

commit v6 on v5

--- a/solution.py
+++ b/solution.py
@@ -11,7 +11,7 @@
 F32 = jnp.float32
 BF16 = jnp.bfloat16
 ROWS = 64
-LOCALS = 13
+LOCALS = 10
 LANDINGS = 26
 GELU_A = 0.7978845608028654
 GELU_B = 0.7978845608028654 * 0.044715
@@ -30,7 +30,7 @@
     seq_devices,
     stream, skip, norm_gain, norm_shift, conv_weight, mid_gain, mid_shift, mix_weight, up_gain, up_shift, up_weight,
     out,
-    xr, a0, hb, mw, cw, uw, a1, x1, h1, eh, ex, eg, ea, uf, outf, zf, cf, accf, skipb, ng, ns, mg, ms, ug, us,
+    xr, a0, hb, mw, cw, uw, a1, x1, h1, eh, ex, eg, ea, uf, outf, zf, cf, accf, skipb, norms, mids, ups,
     local_sem, send_sem, recv_sem, go_sem, known_sem,
 ):
     s = lax.axis_index("seq")
@@ -40,11 +40,7 @@
     sib_s = s + 1 - 2 * core
     crs_s = lax.rem(s + seq_devices - 1 + 2 * core, seq_devices)
     cut_s = lax.rem(s + seq_devices // 2, seq_devices)
-    x_at = lax.rem(s // 2, 4)
     z_bit = lax.rem(s // 8, 2)
-    row = s - 2 * x_at
-    x_next = row + 2 * lax.rem(x_at + 1, 4)
-    x_last = row + 2 * lax.rem(x_at + 3, 4)
     z_step = 8 - 16 * z_bit
     y_bit = s // (seq_devices // 2)
     has_crs = jnp.logical_and(s > 0, s < seq_devices - 1)
@@ -65,7 +61,9 @@
     dcr = {"seq": crs_s, "ch": o}
     dsb = {"seq": sib_s, "ch": o}
     cut = {"seq": cut_s, "ch": o}
-    mates = [{"seq": x_next, "ch": g}, {"seq": x_last, "ch": g}, {"seq": s + z_step, "ch": g}]
+    x_bit = lax.rem(s // 2, 2)
+    x_pair = s + 2 - 4 * x_bit
+    mates = [{"seq": x_pair + z_step, "ch": g}, {"seq": x_pair, "ch": g}, {"seq": s + z_step, "ch": g}]
     partners = [par, sib, cut] + mates
     middle = s // 2 == seq_devices // 4
 
@@ -88,15 +86,22 @@
         local.append(copy)
         return copy
 
+    def fetch_pair(first_src, second_src, dst):
+        both_here = pltpu.make_async_copy(dst, dst, local_sem.at[len(local)])
+        for k, src in enumerate((first_src, second_src)):
+            pltpu.make_async_copy(src, dst.at[k], local_sem.at[len(local)]).start()
+        local.append(both_here)
+
     own_copy = fetch(stream, xr.at[g, 1])
-    gain_copies = [
-        fetch(norm_gain, ng), fetch(norm_shift, ns), fetch(mid_gain, mg), fetch(mid_shift, ms),
-    ]
+    fetch_pair(norm_gain, norm_shift, norms)
+    fetch_pair(mid_gain, mid_shift, mids)
     cw0_copy = fetch(conv_weight.at[0], cw.at[0])
     mw0_copy = fetch(mix_weight.at[0], mw.at[0, g])
     cw1_copy = fetch(conv_weight.at[1], cw.at[1])
     mw1_copy = fetch(mix_weight.at[1], mw.at[1, g])
-    up_copies = [fetch(up_gain, ug), fetch(up_shift, us), fetch(up_weight, uw), fetch(skip, skipb)]
+    up_copies = [fetch(up_weight, uw), fetch(skip, skipb)]
+    fetch_pair(up_gain, up_shift, ups)
+    ng, ns, mg, ms, ug, us = norms.at[0], norms.at[1], mids.at[0], mids.at[1], ups.at[0], ups.at[1]
 
     sends = []
     names = {}
@@ -140,19 +145,18 @@
                 for copy in some:
                     copy.wait_send()
 
-    to_sib = 2 * core
-    to_crs = 2 - 2 * core
-    my_sib = 2 - 2 * core
-    my_crs = 2 * core
+    to_sib = my_sib = 0
+    to_crs = my_crs = 2
+    sib_side = 2 - 2 * core
+    crs_side = 2 * core
     near = pl.ds(pl.multiple_of(32 * core, 32), 32)
     far = pl.ds(pl.multiple_of(32 - 32 * core, 32), 32)
 
-    def piece(shift):
-        quarter = lax.rem(x_at + 2 * z_bit + shift, 4)
-        return pl.ds(pl.multiple_of(128 * core + 32 * quarter, 32), 32)
+    def piece(x, z):
+        return pl.ds(pl.multiple_of(128 * core + 32 * x + 64 * z, 32), 32)
 
     theirs = pl.ds(pl.multiple_of(128 - 128 * core, 128), 128)
-    pieces = [piece(0), piece(3), piece(1), piece(2)]
+    pieces = [piece(x_bit, z_bit), piece(1 - x_bit, 1 - z_bit), piece(1 - x_bit, z_bit), piece(x_bit, 1 - z_bit)]
 
     own_copy.wait()
     entered = len(partners) + has_crs.astype(jnp.int32) + direct.astype(jnp.int32) + middle.astype(jnp.int32)
@@ -186,8 +190,8 @@
         send(f"x_par{b}", xr.at[g, 1, b, near], xr.at[g, 1, b, near], par)
     x_crs = send("x_crs", xr.at[g, 1, :, near], xr.at[g, to_crs, :, near], crs, has_crs, at_once)
     x_dcr = send("x_near", xr.at[g, 1, :, near], xr.at[g, to_crs, :, near], dcr, direct, jnp.logical_and(direct, at_once))
+    send("w_cut0", mix_weight.at[0, pieces[0]], mw.at[0, g, pieces[0]], cut)
     send("x_par2", xr.at[g, 1, :, far], xr.at[g, 1, :, far], par)
-    send("w_cut0", mix_weight.at[0, pieces[0]], mw.at[0, g, pieces[0]], cut)
     send("x_sib", xr.at[g, 1], xr.at[g, to_sib], sib)
     x_crs2 = send("x_far", xr.at[g, 1, :, far], xr.at[g, to_crs, :, far], crs, has_crs, at_once)
     for device in fed:
@@ -220,7 +224,7 @@
     whole = pl.ds(0, ROWS)
     centre = pl.ds(32, ROWS)
 
-    for copy in gain_copies:
+    for copy in local[1:3]:
         copy.wait()
     activate0(g, 1, whole, centre, None)
     arrive("x_sib", xr.at[g, my_sib])
@@ -288,7 +292,7 @@
         arrive(f"w_mate{m}", mw.at[0, o, pieces[m + 1]])
         weights("w_fwd0", 0, pieces[m + 1], sib)
 
-    def mix0(slot, valid, rows, batch):
+    def mix0(slot, tap, valid, rows, batch):
         count = rows.stop - rows.start
         for n in range(4):
             cols = slice(256 * n, 256 * n + 256)
@@ -301,7 +305,7 @@
             if valid is not None:
                 v = jnp.where(valid, v, 0.0)
             a1[slot, rows, cols] = v.astype(BF16)
-        return dot(a1[slot, rows], cw[1, slot])
+        return dot(a1[slot, rows], cw[1, tap])
 
     last = pl.ds(pl.multiple_of(48 - 48 * core, 16), 16)
     first = pl.ds(pl.multiple_of(48 * core, 16), 16)
@@ -318,15 +322,15 @@
         weights(f"w_mate{m + 3}", 1, pieces[0], mates[m])
     weights("w_fwd1", 1, pieces[0], sib)
     arrive("w_fwd0", mw.at[0, o, theirs])
-    acc = mix0(1, None, every, both)
+    acc = mix0(1, 1, None, every, both)
     arrive("h_sib", hb.at[:, my_sib])
     arrive("x_fwd2", xr.at[o, my_sib, :, far])
-    acc = acc + mix0(my_sib, None, every, both)
+    acc = acc + mix0(my_sib, sib_side, None, every, both)
     arrive_if(has_crs, "x_far", xr.at[:, my_crs, :, near])
     for b in range(2):
         rows = slice(ROWS * b, ROWS * b + ROWS)
         arrive_if(has_crs, f"h_crs{b}", hb.at[:, my_crs, rows])
-        part = acc[rows] + mix0(my_crs, has_crs, rows, slice(b, b + 1))
+        part = acc[rows] + mix0(my_crs, crs_side, has_crs, rows, slice(b, b + 1))
         h1[g, b] = gelu(part * mg[1:2, :] + ms[1:2, :]).astype(BF16)
         if b == 1:
             send("x_crs", h1.at[g, :, first], eh.at[g, 1 - core], dcr, direct_edges)
@@ -349,7 +353,7 @@
             ea[:, cols] = gelu(x * ng[1:2, cols] + ns[1:2, cols]).astype(BF16)
         y = dot(ea[...], cw[1, 0])
         for k in range(2):
-            tail = jnp.concatenate([a1[k, ROWS * b + 48 : ROWS * b + ROWS, :] for b in range(2)], axis=0)
+            tail = jnp.concatenate([a1[2 - k, ROWS * b + 48 : ROWS * b + ROWS, :] for b in range(2)], axis=0)
             y = y + dot(tail, cw[1, k + 1])
         eh[g, 0] = gelu(y * mg[1:2, :] + ms[1:2, :]).astype(BF16).reshape(2, 16, 256)
 
@@ -357,12 +361,8 @@
     send("x_crs", eh.at[g, 0], eh.at[g, 0], par, ahead)
 
     mw1_copy.wait()
-    for copy in up_copies:
+    for copy in up_copies + local[-1:]:
         copy.wait()
-
-    edge_rows = [
-        [slice(ROWS * b + 48 - 48 * side, ROWS * b + 64 - 48 * side) for b in range(2)] for side in range(2)
-    ]
 
     def half_top():
         for n in range(4):
@@ -378,17 +378,20 @@
             uf[b, 8 : 8 + ROWS, cols] = v.astype(BF16).astype(F32)
 
     def edge_top():
+        left, right = 2 - 2 * core, 2 * core
         for n in range(4):
             cols = slice(256 * n, 256 * n + 256)
             z = dot(eh[0].reshape(64, 256), mw[1, 0, :, cols]) + dot(eh[1].reshape(64, 256), mw[1, 1, :, cols])
-            base = jnp.concatenate([x1[2 * side, rows, cols] for side in range(2) for rows in edge_rows[side]], axis=0)
-            v = (base.astype(F32) + z).astype(BF16).astype(F32)
-            v = gelu(v * ug[0:1, cols] + us[0:1, cols]).astype(BF16).astype(F32)
             for b in range(2):
-                uf[b, 0:8, cols] = jnp.where(s > 0, v[16 * b + 8 : 16 * b + 16], 0.0)
-                uf[b, 8 + ROWS : 16 + ROWS, cols] = jnp.where(
-                    s < seq_devices - 1, v[32 + 16 * b : 32 + 16 * b + 8], 0.0
-                )
+                for base, part, valid, to in (
+                    (x1[left, ROWS * b + 48 : ROWS * b + ROWS, cols].astype(F32)[8:], z[16 * b + 8 : 16 * b + 16],
+                     s > 0, slice(0, 8)),
+                    (x1[right, ROWS * b : ROWS * b + 16, cols].astype(F32)[:8], z[32 + 16 * b : 40 + 16 * b],
+                     s < seq_devices - 1, slice(8 + ROWS, 16 + ROWS)),
+                ):
+                    v = (base + part).astype(BF16).astype(F32)
+                    v = gelu(v * ug[0:1, cols] + us[0:1, cols]).astype(BF16).astype(F32)
+                    uf[b, to, cols] = jnp.where(valid, v, 0.0)
 
     def rows_at(offset):
         return jnp.concatenate(
@@ -463,12 +466,9 @@
             pltpu.VMEM((4, 128, 256), F32),
             pltpu.VMEM((128, 256), F32),
             pltpu.VMEM((2, 256, 256), BF16),
-            pltpu.VMEM((2, 1024), F32),
-            pltpu.VMEM((2, 1024), F32),
-            pltpu.VMEM((2, 256), F32),
-            pltpu.VMEM((2, 256), F32),
-            pltpu.VMEM((1, 1024), F32),
-            pltpu.VMEM((1, 1024), F32),
+            pltpu.VMEM((2, 2, 1024), F32),
+            pltpu.VMEM((2, 2, 256), F32),
+            pltpu.VMEM((2, 1, 1024), F32),
             pltpu.SemaphoreType.DMA((LOCALS,)),
             pltpu.SemaphoreType.DMA((1,)),
             pltpu.SemaphoreType.DMA((LANDINGS,)),

time: 27.9 us -> 27.3 us (0.978); the launches traced: 27.5 us -> 27.3 us
  no operation moved by 1% of the time
where the time goes in v6:
time: 27.3 us
  Pallas kernels  26.6 us (97%)
  local copies, waits for them, and re-layouts  0.71 us (3%)
    pallas_call x1, Pallas kernels, body(): pl.pallas_call(functools.partial(kernel, seq_devices), name='bottleneck',...  26.6 us
    unnamed x1, local copies, waits for them, and re-layouts  0.71 us

profile of v6, /device:TPU:8, one launch (start us, length us, event | category | flops | bytes accessed | tf_op | source)
XLA Modules:
  0.0 27.3 jit_solution(10024830397282377102)
XLA Ops:
  0.0 26.6 %bottleneck.1 = bf16[2,256,256]{2,1,0:T(8,128)(2,1)S(1)} custom-call(bf16[2,64,512]{2,1,0:T(8,128)(2,1)} %stream.1, bf16[2,256,256]{2,1,0:T(8,128)(2,1)} %skip.1, f32[2,1024]{1,0:T(2,128)} %norm_gain.1, f32[2,1024]{1,0:T(2,128)} %norm_shift.1, bf16[2,3,1024,256]{3,2,1,0:T(8,128)(2,1)} %conv_weight.1, f32[2,256]{1,0:T(2,128)} %mid_gain.1, ...), custom_call_target="tpu_custom_call" | custom-call | tf_op jit(solution)/shard_map/bottleneck/pallas_call | solution.py:443
  26.6 0.7 %copy.13 = bf16[2,256,256]{2,1,0:T(8,128)(2,1)} copy(bf16[2,256,256]{2,1,0:T(8,128)(2,1)S(1)} %bottleneck.1) | data formatting | bytes 524288

commit v7 on v6

--- a/solution.py
+++ b/solution.py
@@ -252,13 +252,13 @@
     accf[...] = conv0(g)
     arrive("x_par2", xr.at[o, 1, :, far])
     send("x_fwd", xr.at[o, 1, :, far], xr.at[o, to_sib, :, far], sib)
-    send("x_far", xr.at[o, 1, :, far], xr.at[o, to_crs, :, far], crs, has_crs)
     send("w_cut1", mix_weight.at[1, pieces[0]], mw.at[1, g, pieces[0]], cut)
     activate0(o, 1, whole, centre, None)
     arrive("w_cut0", mw.at[0, o, pieces[0]])
     for m in range(3):
         weights(f"w_mate{m}", 0, pieces[0], mates[m])
     weights("w_fwd0", 0, pieces[0], sib)
+    send("x_far", xr.at[o, 1, :, far], xr.at[o, to_crs, :, far], crs, has_crs)
     send("x_fwd2", xr.at[o, 1, :, near], xr.at[o, to_sib, :, near], sib)
     arrive("x_fwd", xr.at[o, my_sib, :, near])
     activate0(o, my_sib, sib_src, sib_dst, None)

time: 27.3 us -> 27.3 us (level)
  no operation moved by 1% of the time
where the time goes in v7:
time: 27.3 us
  Pallas kernels  26.6 us (97%)
  local copies, waits for them, and re-layouts  0.71 us (3%)
    pallas_call x1, Pallas kernels, body(): pl.pallas_call(functools.partial(kernel, seq_devices), name='bottleneck',...  26.6 us
    unnamed x1, local copies, waits for them, and re-layouts  0.71 us

profile of v7, /device:TPU:8, one launch (start us, length us, event | category | flops | bytes accessed | tf_op | source)
XLA Modules:
  0.0 27.3 jit_solution(16765288592585641293)
XLA Ops:
  0.0 26.6 %bottleneck.1 = bf16[2,256,256]{2,1,0:T(8,128)(2,1)S(1)} custom-call(bf16[2,64,512]{2,1,0:T(8,128)(2,1)} %stream.1, bf16[2,256,256]{2,1,0:T(8,128)(2,1)} %skip.1, f32[2,1024]{1,0:T(2,128)} %norm_gain.1, f32[2,1024]{1,0:T(2,128)} %norm_shift.1, bf16[2,3,1024,256]{3,2,1,0:T(8,128)(2,1)} %conv_weight.1, f32[2,256]{1,0:T(2,128)} %mid_gain.1, ...), custom_call_target="tpu_custom_call" | custom-call | tf_op jit(solution)/shard_map/bottleneck/pallas_call | solution.py:443
  26.6 0.7 %copy.13 = bf16[2,256,256]{2,1,0:T(8,128)(2,1)} copy(bf16[2,256,256]{2,1,0:T(8,128)(2,1)S(1)} %bottleneck.1) | data formatting | bytes 524288
